TPU v7x, 128 devices: a whole 4x4x4 slice. The times are simulated.
128 devices in a mesh: tm: 4 (over z_hi, core), tile: 32 (over x, y, z_lo).
Axes of the slice: x: 4, y: 4, z: 4 (z_hi: 2, z_lo: 2; z = z_hi * 2 + z_lo), core: 2. Of those that a mesh axis runs over, the one named last changes fastest.
Arguments:
- features: bfloat16 [16, 32, 49152], P('tm', 'tile'), may hold values from -28 to 28
- first_gain: float32 [192], replicated, may hold values from 0.1 to 1.9
- first_kernel: bfloat16 [3, 3, 3, 192, 192], replicated, may hold values from -0.078125 to 0.078125
- first_offset: float32 [192], replicated, may hold values from -3 to 3
- second_gain: float32 [192], replicated, may hold values from 0.1 to 1.9
- second_kernel: bfloat16 [3, 3, 3, 192, 192], replicated, may hold values from -0.078125 to 0.078125
- second_offset: float32 [192], replicated, may hold values from -3 to 3
- upsample_kernel: bfloat16 [3, 3, 192, 96], replicated, may hold values from -0.15625 to 0.15625
- upsample_offset: float32 [96], replicated, may hold values from -3 to 3
Outputs:
- decoded: bfloat16 [16, 64, 49152], P('tm', 'tile')
All inputs are finite; a program needn't handle non-finite values.
Results may differ from a plain program's by a relative error of at most 0.0052.
Values may be sent and summed in bfloat16 or wider, within the bound.
A program may use at most 128 MiB of HBM per device.

v0:
```python
import jax
import jax.numpy as jnp
from jax import lax
from jax.sharding import PartitionSpec as P

epsilon = 1e-06


def with_halo(cells, sides, width):
    for axis, dim in sides:
        count = lax.axis_size(axis)
        ends = count - 1
        head = lax.slice_in_dim(cells, 0, width, axis=dim)
        tail = lax.slice_in_dim(cells, cells.shape[dim] - width, cells.shape[dim], axis=dim)
        cells = jnp.concatenate(
            [
                lax.ppermute(tail, axis, [(i, (i + 1) % count) for i in range(ends)]),
                cells,
                lax.ppermute(head, axis, [((i + 1) % count, i) for i in range(ends)]),
            ],
            axis=dim,
        )
    return cells


def shifted(array, axis, by):
    peers = lax.axis_size(axis)
    pairs = [(i, i + by) for i in range(peers) if 0 <= i + by < peers]
    return lax.ppermute(array, axis, pairs)


def norm_silu(hidden, gain):
    values = hidden.astype(jnp.float32)
    power = jnp.mean(values * values, axis=3, keepdims=True)
    scaled = values * lax.rsqrt(power + epsilon) * gain
    return jax.nn.silu(scaled).astype(jnp.bfloat16)


def causal_conv(stacked, kernel, offset):
    count_in, height, columns, channels = stacked.shape
    frames = count_in - 2
    outgoing = kernel.shape[-1]
    rimmed = with_halo(stacked, (("tile", 1),), 1)
    padded = jnp.pad(rimmed, ((0, 0), (0, 0), (1, 1), (0, 0)))
    widened = jnp.concatenate(
        [padded[:, :, shift_col : shift_col + columns, :] for shift_col in range(3)], axis=3
    )
    result = jnp.zeros((frames * height * columns, outgoing), jnp.float32)
    for temporal in range(3):
        for vertical in range(3):
            window = widened[temporal : temporal + frames, vertical : vertical + height].reshape(
                -1, 3 * channels
            )
            result = result + jnp.dot(
                window,
                kernel[temporal, vertical].reshape(3 * channels, outgoing),
                preferred_element_type=jnp.float32,
            )
    return result.reshape(frames, height, columns, outgoing) + offset


def carried(active):
    return shifted(active[active.shape[0] - 2 :], "tm", 1)


def upsample_conv(lowres, kernel, offset):
    frames, height, columns, channels = lowres.shape
    outgoing = kernel.shape[-1]
    doubled = jnp.repeat(jnp.repeat(lowres, 2, axis=1), 2, axis=2)
    rimmed = with_halo(doubled, (("tile", 1),), 1)
    padded = jnp.pad(rimmed, ((0, 0), (0, 0), (1, 1), (0, 0)))
    widened = jnp.concatenate(
        [padded[:, :, shift_col : shift_col + 2 * columns, :] for shift_col in range(3)], axis=3
    )
    result = jnp.zeros((frames * 2 * height * 2 * columns, outgoing), jnp.float32)
    for vertical in range(3):
        window = widened[:, vertical : vertical + 2 * height].reshape(-1, 3 * channels)
        result = result + jnp.dot(
            window,
            kernel[vertical].reshape(3 * channels, outgoing),
            preferred_element_type=jnp.float32,
        )
    return (
        (result + offset).astype(jnp.bfloat16).reshape(frames, 2 * height, 2 * columns * outgoing)
    )


def shards(
    features,
    first_gain,
    first_kernel,
    first_offset,
    second_gain,
    second_kernel,
    second_offset,
    upsample_kernel,
    upsample_offset,
):
    frames, height, flat_width = features.shape
    channels = first_kernel.shape[3]
    columns = flat_width // channels
    inputs = features.reshape(frames, height, columns, channels)
    first_act = norm_silu(inputs, first_gain)
    hidden_one = causal_conv(
        jnp.concatenate([carried(first_act), first_act], axis=0), first_kernel, first_offset
    )
    second_act = norm_silu(hidden_one, second_gain)
    hidden_two = causal_conv(
        jnp.concatenate([carried(second_act), second_act], axis=0), second_kernel, second_offset
    )
    merged = (inputs.astype(jnp.float32) + hidden_two).astype(jnp.bfloat16)
    return upsample_conv(merged, upsample_kernel, upsample_offset)


def solution(mesh):
    placed = (P("tm", "tile", None), P(), P(), P(), P(), P(), P(), P(), P())
    return jax.shard_map(
        shards, mesh=mesh, in_specs=placed, out_specs=P("tm", "tile", None), check_vma=False
    )
```

profile of v0, /device:TPU:7, one launch (start us, length us, event | category | flops | bytes accessed | tf_op | source)
XLA Modules:
  0.0 175.5 jit_solution(9961921769628858701)
XLA Ops:
  0.0 1.5 reshape.262
  2.1 6.1 %collective-permute-start = (bf16[2,1,256,192]{3,2,0,1:T(8,128)(2,1)S(1)}, bf16[2,1,256,192]{3,2,0,1:T(8,128)(2,1)S(1)}, u32[]{:S(2)}, u32[]{:S(2)}) collective-permute-start(bf16[2,1,256,192]{3,2,0,1:T(8,128)(2,1)S(1)} %slice.208), channel_id=1, source_target_pairs={{0,32},{32,64},{64,96},{1,33},{33,65},{65,97},{2,34},{34,66},{66,9... | collective-permute-start | bytes 589832 | tf_op jit(solution)/shard_map/ppermute | solution.py:29
  8.2 4.1 %collective-permute-done = bf16[2,1,256,192]{3,2,0,1:T(8,128)(2,1)S(1)} collective-permute-done((bf16[2,1,256,192]{3,2,0,1:T(8,128)(2,1)S(1)}, bf16[2,1,256,192]{3,2,0,1:T(8,128)(2,1)S(1)}, u32[]{:S(2)}, u32[]{:S(2)}) %collective-permute-start) | collective-permute-done | bytes 196640 | tf_op jit(solution)/shard_map/ppermute | solution.py:29
  12.7 1.9 %collective-permute-start.1 = (bf16[6,1,256,192]{2,3,1,0:T(8,128)(2,1)S(1)}, bf16[6,1,256,192]{2,3,1,0:T(8,128)(2,1)}, u32[]{:S(2)}, u32[]{:S(2)}) collective-permute-start(bf16[6,1,256,192]{2,3,1,0:T(8,128)(2,1)S(1)} %copy.56), channel_id=1, source_target_pairs={{0,1},{1,2},{2,3},{3,4},{4,5},{5,6},{6,7},{7,8},{8,9},{9,10},{10,1... | collective-permute-start | bytes 1769480 | tf_op jit(solution)/shard_map/ppermute | solution.py:17
  14.6 11.6 %collective-permute-start.2 = (bf16[6,1,256,192]{2,3,1,0:T(8,128)(2,1)S(1)}, bf16[6,1,256,192]{2,3,1,0:T(8,128)(2,1)}, u32[]{:S(2)}, u32[]{:S(2)}) collective-permute-start(bf16[6,1,256,192]{2,3,1,0:T(8,128)(2,1)S(1)} %copy.56), channel_id=1, source_target_pairs={{1,0},{2,1},{3,2},{4,3},{5,4},{6,5},{7,6},{8,7},{9,8},{10,9},{11,1... | collective-permute-start | bytes 1769480 | tf_op jit(solution)/shard_map/ppermute | solution.py:19
  26.2 2.8 %fusion.40 = (bf16[1,1,3,192,192]{4,3,2,1,0:T(8,128)(2,1)S(1)}, bf16[1,1,3,192,192]{4,3,2,1,0:T(8,128)(2,1)S(1)}, bf16[1,1,3,192,192]{4,3,2,1,0:T(8,128)(2,1)}, ...) fusion(bf16[3,3,3,192,192]{4,3,2,1,0:T(8,128)(2,1)} %param.11), kind=kLoop, calls=%fused_computation.62 | loop fusion | bytes 3981312 | tf_op jit(solution)/shard_map/slice | solution.py:56
  29.0 2.7 %collective-permute-done.1 = bf16[6,1,256,192]{2,3,1,0:T(8,128)(2,1)} collective-permute-done((bf16[6,1,256,192]{2,3,1,0:T(8,128)(2,1)S(1)}, bf16[6,1,256,192]{2,3,1,0:T(8,128)(2,1)}, u32[]{:S(2)}, u32[]{:S(2)}) %collective-permute-start.1) | collective-permute-done | bytes 589856 | tf_op jit(solution)/shard_map/ppermute | solution.py:17
  31.8 1.3 copy.58
  33.1 6.3 %collective-permute-done.2 = bf16[6,1,256,192]{2,3,1,0:T(8,128)(2,1)} collective-permute-done((bf16[6,1,256,192]{2,3,1,0:T(8,128)(2,1)S(1)}, bf16[6,1,256,192]{2,3,1,0:T(8,128)(2,1)}, u32[]{:S(2)}, u32[]{:S(2)}) %collective-permute-start.2) | collective-permute-done | bytes 589856 | tf_op jit(solution)/shard_map/ppermute | solution.py:19
  39.4 1.3 copy.59
  40.8 1.1 fusion.16
  41.9 1.5 fusion.42
  43.3 4.2 %pad_maximum_fusion.1 = bf16[6,3,256,576]{3,2,0,1:T(8,128)(2,1)S(1)} fusion(bf16[6,3,256,192]{3,2,0,1:T(8,128)(2,1)S(1)} %get-tuple-element.49, bf16[6,1,256,192]{3,2,0,1:T(8,128)(2,1)S(1)} %copy.59, bf16[4,1,256,192]{3,2,0,1:T(8,128)(2,1)S(1)} %multiply_convert_fusion.1, bf16[2,1,256,192]{3,2,0,1:T(8,128)(2,1)S(1)} %collective-permute-done, ...), kind=kLoop, calls=%fused_computation.6 | loop fusion | flops 31850496 | bytes 10616832 | tf_op jit(solution)/shard_map/concatenate | solution.py:45
  47.5 1.7 fusion.37
  49.3 0.6 fusion.44
  50.3 0.6 fusion.45
  50.9 0.6 fusion.46
  51.5 0.6 fusion.47
  52.2 0.6 fusion.48
  52.8 0.6 fusion.49
  53.4 0.6 fusion.50
  54.0 0.6 fusion.51
  54.7 0.9 multiply_reduce_fusion.1
  56.4 5.5 %collective-permute-start.3 = (bf16[2,1,256,192]{3,2,0,1:T(8,128)(2,1)S(1)}, bf16[2,1,256,192]{3,2,0,1:T(8,128)(2,1)S(1)}, u32[]{:S(2)}, u32[]{:S(2)}) collective-permute-start(bf16[2,1,256,192]{3,2,0,1:T(8,128)(2,1)S(1)} %slice.220), channel_id=1, source_target_pairs={{0,32},{32,64},{64,96},{1,33},{33,65},{65,97},{2,34},{34,66},{66,9... | collective-permute-start | bytes 589832 | tf_op jit(solution)/shard_map/ppermute | solution.py:29
  61.8 3.9 %collective-permute-done.3 = bf16[2,1,256,192]{3,2,0,1:T(8,128)(2,1)S(1)} collective-permute-done((bf16[2,1,256,192]{3,2,0,1:T(8,128)(2,1)S(1)}, bf16[2,1,256,192]{3,2,0,1:T(8,128)(2,1)S(1)}, u32[]{:S(2)}, u32[]{:S(2)}) %collective-permute-start.3) | collective-permute-done | bytes 196640 | tf_op jit(solution)/shard_map/ppermute | solution.py:29
  65.9 1.1 copy.61
  67.0 3.1 %collective-permute-start.4 = (bf16[6,1,256,192]{2,3,1,0:T(8,128)(2,1)}, bf16[6,1,256,192]{2,3,1,0:T(8,128)(2,1)}, u32[]{:S(2)}, u32[]{:S(2)}) collective-permute-start(bf16[6,1,256,192]{2,3,1,0:T(8,128)(2,1)} %copy.61), channel_id=1, source_target_pairs={{0,1},{1,2},{2,3},{3,4},{4,5},{5,6},{6,7},{7,8},{8,9},{9,10},{10,1... | collective-permute-start | bytes 1769480 | tf_op jit(solution)/shard_map/ppermute | solution.py:17
  70.1 5.4 %collective-permute-start.5 = (bf16[6,1,256,192]{2,3,1,0:T(8,128)(2,1)}, bf16[6,1,256,192]{2,3,1,0:T(8,128)(2,1)}, u32[]{:S(2)}, u32[]{:S(2)}) collective-permute-start(bf16[6,1,256,192]{2,3,1,0:T(8,128)(2,1)} %copy.61), channel_id=1, source_target_pairs={{1,0},{2,1},{3,2},{4,3},{5,4},{6,5},{7,6},{8,7},{9,8},{10,9},{11,1... | collective-permute-start | bytes 1769480 | tf_op jit(solution)/shard_map/ppermute | solution.py:19
  75.5 0.5 reshape.261
  76.3 3.1 %fusion.39 = (bf16[1,1,3,192,192]{4,3,2,1,0:T(8,128)(2,1)S(1)}, bf16[1,1,3,192,192]{4,3,2,1,0:T(8,128)(2,1)}, bf16[1,1,3,192,192]{4,3,2,1,0:T(8,128)(2,1)}, bf16...) fusion(bf16[3,3,3,192,192]{4,3,2,1,0:T(8,128)(2,1)} %param.14), kind=kLoop, calls=%fused_computation.61 | loop fusion | bytes 3981312 | tf_op jit(solution)/shard_map/slice | solution.py:56
  79.4 4.8 %collective-permute-done.4 = bf16[6,1,256,192]{2,3,1,0:T(8,128)(2,1)} collective-permute-done((bf16[6,1,256,192]{2,3,1,0:T(8,128)(2,1)}, bf16[6,1,256,192]{2,3,1,0:T(8,128)(2,1)}, u32[]{:S(2)}, u32[]{:S(2)}) %collective-permute-start.4) | collective-permute-done | bytes 589856 | tf_op jit(solution)/shard_map/ppermute | solution.py:17
  84.2 1.3 copy.63
  85.5 9.2 %collective-permute-done.5 = bf16[6,1,256,192]{2,3,1,0:T(8,128)(2,1)} collective-permute-done((bf16[6,1,256,192]{2,3,1,0:T(8,128)(2,1)}, bf16[6,1,256,192]{2,3,1,0:T(8,128)(2,1)}, u32[]{:S(2)}, u32[]{:S(2)}) %collective-permute-start.5) | collective-permute-done | bytes 589856 | tf_op jit(solution)/shard_map/ppermute | solution.py:19
  94.7 1.3 copy.64
  96.1 1.1 select_maximum_fusion
  97.1 1.5 fusion.41
  98.6 4.2 %pad_maximum_fusion.2 = bf16[6,3,256,576]{3,2,0,1:T(8,128)(2,1)S(1)} fusion(bf16[6,3,256,192]{3,2,0,1:T(8,128)(2,1)S(1)} %get-tuple-element.47, bf16[6,1,256,192]{3,2,0,1:T(8,128)(2,1)S(1)} %copy.64, bf16[4,1,256,192]{3,2,0,1:T(8,128)(2,1)S(1)} %multiply_convert_fusion, bf16[2,1,256,192]{3,2,0,1:T(8,128)(2,1)S(1)} %collective-permute-done.3, ...), kind=kLoop, calls=%fused_computation.7 | loop fusion | flops 31850496 | bytes 10616832 | tf_op jit(solution)/shard_map/concatenate | solution.py:45
  102.8 1.7 fusion.36
  104.6 0.6 fusion.52
  105.6 0.6 fusion.53
  106.2 0.6 fusion.54
  106.8 0.6 fusion.55
  107.5 0.6 fusion.56
  108.1 0.6 fusion.57
  108.8 0.6 fusion.58
  109.4 0.6 fusion.59
  110.0 0.8 fusion.25
  111.6 0.7 copy.68
  112.3 8.6 %collective-permute-start.6 = (bf16[4,1,512,192]{2,3,1,0:T(8,128)(2,1)S(1)}, bf16[4,1,512,192]{2,3,1,0:T(8,128)(2,1)}, u32[]{:S(2)}, u32[]{:S(2)}) collective-permute-start(bf16[4,1,512,192]{2,3,1,0:T(8,128)(2,1)S(1)} %copy.68), channel_id=1, source_target_pairs={{0,1},{1,2},{2,3},{3,4},{4,5},{5,6},{6,7},{7,8},{8,9},{9,10},{10,1... | collective-permute-start | bytes 2359304 | tf_op jit(solution)/shard_map/ppermute | solution.py:17
  120.9 2.1 %collective-permute-start.7 = (bf16[4,1,512,192]{2,3,1,0:T(8,128)(2,1)S(1)}, bf16[4,1,512,192]{2,3,1,0:T(8,128)(2,1)}, u32[]{:S(2)}, u32[]{:S(2)}) collective-permute-start(bf16[4,1,512,192]{2,3,1,0:T(8,128)(2,1)S(1)} %copy.68), channel_id=1, source_target_pairs={{1,0},{2,1},{3,2},{4,3},{5,4},{6,5},{7,6},{8,7},{9,8},{10,9},{11,1... | collective-permute-start | bytes 2359304 | tf_op jit(solution)/shard_map/ppermute | solution.py:19
  123.1 0.7 fusion.43
  123.9 25.1 %collective-permute-done.6 = bf16[4,1,512,192]{2,3,1,0:T(8,128)(2,1)} collective-permute-done((bf16[4,1,512,192]{2,3,1,0:T(8,128)(2,1)S(1)}, bf16[4,1,512,192]{2,3,1,0:T(8,128)(2,1)}, u32[]{:S(2)}, u32[]{:S(2)}) %collective-permute-start.6) | collective-permute-done | bytes 786464 | tf_op jit(solution)/shard_map/ppermute | solution.py:17
  149.0 1.4 copy.71
  150.5 2.8 %collective-permute-done.7 = bf16[4,1,512,192]{2,3,1,0:T(8,128)(2,1)} collective-permute-done((bf16[4,1,512,192]{2,3,1,0:T(8,128)(2,1)S(1)}, bf16[4,1,512,192]{2,3,1,0:T(8,128)(2,1)}, u32[]{:S(2)}, u32[]{:S(2)}) %collective-permute-start.7) | collective-permute-done | bytes 786464 | tf_op jit(solution)/shard_map/ppermute | solution.py:19
  153.2 1.4 copy.72
  154.8 1.5 fusion.8
  156.3 1.5 fusion.38
  157.8 6.5 %pad_maximum_fusion = bf16[4,4,512,576]{3,2,1,0:T(8,128)(2,1)S(1)} fusion(bf16[4,4,512,192]{3,2,1,0:T(8,128)(2,1)S(1)} %get-tuple-element.27, bf16[4,1,512,192]{3,2,1,0:T(8,128)(2,1)S(1)} %copy.72, bf16[4,2,512,192]{3,2,1,0:T(8,128)(2,1)S(1)} %broadcast_in_dim.8, bf16[4,1,512,192]{3,2,1,0:T(8,128)(2,1)S(1)} %copy.71, ...), kind=kLoop, calls=%fused_computation.2 | loop fusion | flops 47185920 | bytes 18874368 | tf_op jit(solution)/shard_map/concatenate | solution.py:72
  164.3 2.4 %fusion.35 = (bf16[4,2,512,576]{3,2,1,0:T(8,128)(2,1)S(1)}, bf16[4,2,512,576]{3,2,1,0:T(8,128)(2,1)S(1)}, bf16[4,2,512,576]{3,2,1,0:T(8,128)(2,1)S(1)}) fusion(bf16[4,4,512,576]{3,2,1,0:T(8,128)(2,1)S(1)} %pad_maximum_fusion), kind=kLoop, calls=%fused_computation.57 | loop fusion | bytes 28311552 | tf_op jit(solution)/shard_map/slice | solution.py:77
  166.7 1.8 fusion.60
  168.5 1.8 %convolution_add_fusion.1 = f32[4096,96]{0,1:T(8,128)S(1)} fusion(f32[4096,96]{0,1:T(8,128)S(1)} %fusion.60, bf16[4096,576]{1,0:T(8,128)(2,1)S(1)} %bitcast.99, bf16[576,96]{1,0:T(8,128)(2,1)S(1)} %bitcast.141), kind=kOutput, calls=%fused_computation.13 | convolution fusion | flops 453378048 | bytes 7974912 | tf_op jit(solution)/shard_map/dot_general | solution.py:78
  170.3 1.8 %fusion.6 = bf16[4096,96]{0,1:T(8,128)(2,1)S(1)} fusion(f32[4096,96]{0,1:T(8,128)S(1)} %convolution_add_fusion.1, bf16[4096,576]{1,0:T(8,128)(2,1)S(1)} %bitcast.98, bf16[576,96]{1,0:T(8,128)(2,1)S(1)} %bitcast.143, f32[96]{0:T(128)S(1)} %copy-done.17), kind=kOutput, calls=%fused_computation.15 | convolution fusion | flops 454164480 | bytes 7188864 | tf_op jit(solution)/shard_map/dot_general | solution.py:78
  172.1 0.7 copy.73
  172.7 2.7 %reshape.260 = bf16[4,2,49152]{2,1,0:T(2,128)(2,1)} reshape(bf16[4096,96]{1,0:T(8,128)(2,1)S(1)} %copy.73) | data formatting | bytes 1572864 | tf_op jit(solution)/shard_map/reshape | solution.py:84
  (60 shorter events, 3.9 us)
Async XLA Ops:
  0.0 1.7 copy-start.20
  2.1 10.2 %collective-permute-start = (bf16[2,1,256,192]{3,2,0,1:T(8,128)(2,1)S(1)}, bf16[2,1,256,192]{3,2,0,1:T(8,128)(2,1)S(1)}, u32[]{:S(2)}, u32[]{:S(2)}) collective-permute-start(bf16[2,1,256,192]{3,2,0,1:T(8,128)(2,1)S(1)} %slice.208), channel_id=1, source_target_pairs={{0,32},{32,64},{64,96},{1,33},{33,65},{65,97},{2,34},{34,66},{66,9... | collective-permute-start | bytes 589832 | tf_op jit(solution)/shard_map/ppermute | solution.py:29
  12.7 19.1 %collective-permute-start.1 = (bf16[6,1,256,192]{2,3,1,0:T(8,128)(2,1)S(1)}, bf16[6,1,256,192]{2,3,1,0:T(8,128)(2,1)}, u32[]{:S(2)}, u32[]{:S(2)}) collective-permute-start(bf16[6,1,256,192]{2,3,1,0:T(8,128)(2,1)S(1)} %copy.56), channel_id=1, source_target_pairs={{0,1},{1,2},{2,3},{3,4},{4,5},{5,6},{6,7},{7,8},{8,9},{9,10},{10,1... | collective-permute-start | bytes 1769480 | tf_op jit(solution)/shard_map/ppermute | solution.py:17
  14.6 24.8 %collective-permute-start.2 = (bf16[6,1,256,192]{2,3,1,0:T(8,128)(2,1)S(1)}, bf16[6,1,256,192]{2,3,1,0:T(8,128)(2,1)}, u32[]{:S(2)}, u32[]{:S(2)}) collective-permute-start(bf16[6,1,256,192]{2,3,1,0:T(8,128)(2,1)S(1)} %copy.56), channel_id=1, source_target_pairs={{1,0},{2,1},{3,2},{4,3},{5,4},{6,5},{7,6},{8,7},{9,8},{10,9},{11,1... | collective-permute-start | bytes 1769480 | tf_op jit(solution)/shard_map/ppermute | solution.py:19
  47.5 1.8 %copy-start.12 = (bf16[1,1,3,192,192]{4,3,2,1,0:T(8,128)(2,1)S(1)}, bf16[1,1,3,192,192]{4,3,2,1,0:T(8,128)(2,1)}, u32[]{:S(2)}) copy-start(bf16[1,1,3,192,192]{4,3,2,1,0:T(8,128)(2,1)} %get-tuple-element.43) | copy-start | bytes 663556
  49.3 1.0 copy-start.10
  49.3 1.6 copy-start.8
  49.9 1.6 copy-start.6
  50.9 1.3 copy-start.4
  53.4 1.3 copy-start.16
  54.7 1.3 copy-start.19
  56.0 19.5 %copy-start = (bf16[4,1,49152]{2,0,1:T(4,128)(2,1)S(1)}, bf16[4,1,49152]{2,0,1:T(4,128)(2,1)}, u32[]{:S(2)}) copy-start(bf16[4,1,49152]{2,0,1:T(4,128)(2,1)} %param.9) | copy-start | bytes 1179652
  56.4 9.4 %collective-permute-start.3 = (bf16[2,1,256,192]{3,2,0,1:T(8,128)(2,1)S(1)}, bf16[2,1,256,192]{3,2,0,1:T(8,128)(2,1)S(1)}, u32[]{:S(2)}, u32[]{:S(2)}) collective-permute-start(bf16[2,1,256,192]{3,2,0,1:T(8,128)(2,1)S(1)} %slice.220), channel_id=1, source_target_pairs={{0,32},{32,64},{64,96},{1,33},{33,65},{65,97},{2,34},{34,66},{66,9... | collective-permute-start | bytes 589832 | tf_op jit(solution)/shard_map/ppermute | solution.py:29
  67.0 17.2 %collective-permute-start.4 = (bf16[6,1,256,192]{2,3,1,0:T(8,128)(2,1)}, bf16[6,1,256,192]{2,3,1,0:T(8,128)(2,1)}, u32[]{:S(2)}, u32[]{:S(2)}) collective-permute-start(bf16[6,1,256,192]{2,3,1,0:T(8,128)(2,1)} %copy.61), channel_id=1, source_target_pairs={{0,1},{1,2},{2,3},{3,4},{4,5},{5,6},{6,7},{7,8},{8,9},{9,10},{10,1... | collective-permute-start | bytes 1769480 | tf_op jit(solution)/shard_map/ppermute | solution.py:17
  70.1 24.6 %collective-permute-start.5 = (bf16[6,1,256,192]{2,3,1,0:T(8,128)(2,1)}, bf16[6,1,256,192]{2,3,1,0:T(8,128)(2,1)}, u32[]{:S(2)}, u32[]{:S(2)}) collective-permute-start(bf16[6,1,256,192]{2,3,1,0:T(8,128)(2,1)} %copy.61), channel_id=1, source_target_pairs={{1,0},{2,1},{3,2},{4,3},{5,4},{6,5},{7,6},{8,7},{9,8},{10,9},{11,1... | collective-permute-start | bytes 1769480 | tf_op jit(solution)/shard_map/ppermute | solution.py:19
  102.8 1.8 %copy-start.13 = (bf16[1,1,3,192,192]{4,3,2,1,0:T(8,128)(2,1)S(1)}, bf16[1,1,3,192,192]{4,3,2,1,0:T(8,128)(2,1)}, u32[]{:S(2)}) copy-start(bf16[1,1,3,192,192]{4,3,2,1,0:T(8,128)(2,1)} %get-tuple-element.34) | copy-start | bytes 663556
  104.6 1.0 copy-start.11
  104.6 1.6 copy-start.9
  105.2 1.6 copy-start.7
  106.2 1.3 copy-start.5
  106.8 1.3 copy-start.3
  107.5 1.3 copy-start.2
  108.1 1.3 copy-start.1
  110.0 0.8 copy-start.18
  111.0 12.0 %copy-start.15 = (bf16[3,3,192,96]{3,2,1,0:T(8,128)(2,1)S(1)}, bf16[3,3,192,96]{3,2,1,0:T(8,128)(2,1)}, u32[]{:S(2)}) copy-start(bf16[3,3,192,96]{3,2,1,0:T(8,128)(2,1)} %param.16) | copy-start | bytes 995332
  112.3 36.7 %collective-permute-start.6 = (bf16[4,1,512,192]{2,3,1,0:T(8,128)(2,1)S(1)}, bf16[4,1,512,192]{2,3,1,0:T(8,128)(2,1)}, u32[]{:S(2)}, u32[]{:S(2)}) collective-permute-start(bf16[4,1,512,192]{2,3,1,0:T(8,128)(2,1)S(1)} %copy.68), channel_id=1, source_target_pairs={{0,1},{1,2},{2,3},{3,4},{4,5},{5,6},{6,7},{7,8},{8,9},{9,10},{10,1... | collective-permute-start | bytes 2359304 | tf_op jit(solution)/shard_map/ppermute | solution.py:17
  120.9 32.3 %collective-permute-start.7 = (bf16[4,1,512,192]{2,3,1,0:T(8,128)(2,1)S(1)}, bf16[4,1,512,192]{2,3,1,0:T(8,128)(2,1)}, u32[]{:S(2)}, u32[]{:S(2)}) collective-permute-start(bf16[4,1,512,192]{2,3,1,0:T(8,128)(2,1)S(1)} %copy.68), channel_id=1, source_target_pairs={{1,0},{2,1},{3,2},{4,3},{5,4},{6,5},{7,6},{8,7},{9,8},{10,9},{11,1... | collective-permute-start | bytes 2359304 | tf_op jit(solution)/shard_map/ppermute | solution.py:19
  168.5 1.8 %copy-start.14 = (bf16[1,3,192,96]{3,2,1,0:T(8,128)(2,1)S(1)}, bf16[1,3,192,96]{3,2,1,0:T(8,128)(2,1)}, u32[]{:S(2)}) copy-start(bf16[1,3,192,96]{3,2,1,0:T(8,128)(2,1)} %get-tuple-element.50) | copy-start | bytes 331780
  168.5 1.8 %copy-start.17 = (f32[96]{0:T(128)S(1)}, f32[96]{0:T(128)}, u32[]{:S(2)}) copy-start(f32[96]{0:T(128)} %param.17) | copy-start | bytes 1156
where the time goes:
time: 176 us; the launch traced here: 175 us
  waiting for transfers between devices  59 us (34%)
  starting transfers between devices  44.2 us (25%)
  local copies, waits for them, and re-layouts  34.7 us (20%)
  other arithmetic  19.9 us (11%)
  matrix products  16.8 us (10%)
    ppermute x3, waiting for transfers between devices, with_halo(): lax.ppermute(tail, axis, [(i, (i + 1) % count) for i in range(ends)])  32.7 us
    ppermute x3, starting transfers between devices, with_halo(): lax.ppermute(head, axis, [((i + 1) % count, i) for i in range(ends)])  19.1 us
    ppermute x3, waiting for transfers between devices, with_halo(): lax.ppermute(head, axis, [((i + 1) % count, i) for i in range(ends)])  18.3 us
    ppermute x3, starting transfers between devices, with_halo(): lax.ppermute(tail, axis, [(i, (i + 1) % count) for i in range(ends)])  13.6 us
    ppermute x2, starting transfers between devices, shifted(): return lax.ppermute(array, axis, pairs)  11.5 us
    dot_general x18, matrix products, causal_conv(): jnp.dot(window, kernel[temporal, vertical].reshape(3 * channels, outgoing...  11.5 us
    concatenate x2, other arithmetic, causal_conv(): jnp.concatenate([padded[:, :, shift_col:shift_col + columns, :] for shift...  8.37 us
    ppermute x2, waiting for transfers between devices, shifted(): return lax.ppermute(array, axis, pairs)  8.03 us
  transfers between devices with their start and end apart: 8, of which 8 were waited for; matrix products, arithmetic and copies ran while one was open for 7% of the time, Pallas kernels for 0%

commit v1 on v0

v1 whole, which is shorter than its diff:
```python
import functools

import jax
import jax.numpy as jnp
from jax import lax
from jax.experimental import pallas as pl
from jax.experimental.pallas import tpu as pltpu
from jax.sharding import PartitionSpec as P

MESH = pl.DeviceIdType.MESH
EPS = 1e-06
F32 = jnp.float32
BF16 = jnp.bfloat16
PAIRS = 48
ACT1 = (6, 28, 42)
CONV1 = (7, 26, 41)
CONV2 = (7, 25, 41)
UPS = (8, 24, 40)
N = len(UPS) - 1
WINDOW = 40
SRC_PAIR = (0, 28, 60, 88)
DST_PAIR = (8, 4, 4, 0)


def pair_norm_silu(x0, x1, x2, gain, inside):
    low = lax.broadcasted_iota(jnp.int32, x1.shape, 1) < 64
    s1 = x1 * x1
    even = jnp.sum(x0 * x0 + jnp.where(low, s1, 0.0), axis=1, keepdims=True)
    odd = jnp.sum(x2 * x2 + jnp.where(low, 0.0, s1), axis=1, keepdims=True)
    even = lax.rsqrt(even * (1.0 / 192.0) + EPS)
    odd = lax.rsqrt(odd * (1.0 / 192.0) + EPS)
    scales = (even, jnp.where(low, even, odd), odd)
    outs = []
    for i, (x, s) in enumerate(zip((x0, x1, x2), scales)):
        v = x * s * gain[:, 128 * i : 128 * (i + 1)]
        v = v / (1.0 + jnp.exp(-v))
        outs.append(jnp.where(inside, v, 0.0).astype(BF16))
    return outs


def kernel(
    x_ref, w1_ref, w2_ref, uk_ref, vec_ref, out_ref,
    inb, xin, p1, p2, p3, we1, wo1, we2, wo2, ue, uo, fbuf, stage,
    in_send, in_recv, row_send, row_recv, out_send, out_recv, w_sem,
):
    tm = lax.axis_index("tm")
    tile = lax.axis_index("tile")
    zh, core = tm // 2, tm % 2
    big, zl = tile // 2, tile % 2
    z = zh * 2 + zl
    row = big * 2 + core
    has_up = row > 0
    has_down = row < 31

    def holder(r):
        return (zh * 2 + r % 2, (r // 2) * 2 + zl)

    barrier = pltpu.get_barrier_semaphore()
    for zz in range(4):
        for cc in range(2):
            partner = ((zl == cc) | (core == zz % 2)) & ~((z == zz) & (core == cc))

            @pl.when(partner)
            def _():
                pl.semaphore_signal(
                    barrier, inc=1, device_id=((zz // 2) * 2 + cc, big * 2 + zz % 2), device_id_type=MESH
                )

    outer = jnp.where(core == 1, row + 1, row - 1)
    has_outer = (outer >= 0) & (outer < 32)

    @pl.when(has_outer)
    def _():
        pl.semaphore_signal(barrier, inc=1, device_id=holder(outer), device_id_type=MESH)

    loads = [
        pltpu.make_async_copy(w1_ref, wo1.at[:, :, pl.ds(0, 576)], w_sem.at[0]),
        pltpu.make_async_copy(w1_ref.at[:, :, pl.ds(192, 384)], we1.at[:, :, pl.ds(0, 384)], w_sem.at[1]),
        pltpu.make_async_copy(w1_ref.at[:, :, pl.ds(0, 192)], we1.at[:, :, pl.ds(448, 192)], w_sem.at[2]),
        pltpu.make_async_copy(w2_ref, wo2.at[:, :, pl.ds(0, 576)], w_sem.at[3]),
        pltpu.make_async_copy(w2_ref.at[:, :, pl.ds(192, 384)], we2.at[:, :, pl.ds(0, 384)], w_sem.at[4]),
        pltpu.make_async_copy(w2_ref.at[:, :, pl.ds(0, 192)], we2.at[:, :, pl.ds(448, 192)], w_sem.at[5]),
    ]
    for load in loads:
        load.start()

    pl.semaphore_wait(barrier, jnp.where(zl == core, 5, 6) + has_outer.astype(jnp.int32))

    def reshard(zz):
        src = x_ref.at[pl.ds(12 * SRC_PAIR[zz], 12 * WINDOW)]
        dst = inb.at[tm, pl.ds(12 * DST_PAIR[zz], 12 * WINDOW)]
        local = pltpu.make_async_copy(src, dst, in_recv.at[tm])
        remote = pltpu.make_async_remote_copy(
            src_ref=src, dst_ref=dst, send_sem=in_send.at[zz], recv_sem=in_recv.at[tm],
            device_id=((zz // 2) * 2 + zl, big * 2 + zz % 2), device_id_type=MESH,
        )
        return (z == zz) & (zl == core), local, remote

    for zz in range(4):
        mine, local, remote = reshard(zz)
        pl.when(mine)(local.start)
        pl.when(~mine)(remote.start)

    zeros64 = jnp.zeros((3, 3, 64, 192), BF16)
    we1[:, :, 384:448] = zeros64
    wo1[:, :, 576:640] = zeros64
    we2[:, :, 384:448] = zeros64
    wo2[:, :, 576:640] = zeros64
    for buf in (p2, p3):
        for b in (6, 41):
            buf[:, 16 * b : 16 * b + 16] = jnp.zeros((3, 16, 384), BF16)

    @pl.when(~has_up)
    def _():
        for buf in (p1, p2, p3):
            buf[0] = jnp.zeros((16 * PAIRS, 384), BF16)

    @pl.when(~has_down)
    def _():
        for buf in (p1, p2, p3):
            buf[2] = jnp.zeros((16 * PAIRS, 384), BF16)

    src_lane = lax.broadcasted_iota(jnp.int32, (96, 256), 0)
    dst_lane = lax.broadcasted_iota(jnp.int32, (96, 256), 1)
    for u_ref, shift in ((ue, 0), (uo, 64)):
        sel_a = jnp.where(dst_lane == src_lane + shift, 1.0, 0.0).astype(BF16)
        sel_b = jnp.where(dst_lane == src_lane + shift + 96, 1.0, 0.0).astype(BF16)
        parts = []
        for q in range(3):
            a = [jnp.dot(uk_ref[q, s], sel_a, preferred_element_type=F32) for s in range(3)]
            b = [jnp.dot(uk_ref[q, s], sel_b, preferred_element_type=F32) for s in range(3)]
            parts.append((a[0], a[1] + a[2] + b[0] + b[1], b[2]))
        for phase, tap, rows in ((0, 0, (0,)), (0, 1, (1, 2)), (1, 0, (0, 1)), (1, 1, (2,))):
            left, mid, right = [
                functools.reduce(lambda m, n: m + n, [parts[q][i] for q in rows]).astype(BF16) for i in range(3)
            ]
            base = 640 * tap
            blank = jnp.zeros((64, 256), BF16)
            order = (mid, right, blank, left) if shift == 0 else (left, mid, right, blank)
            for block in order:
                u_ref[phase, base : base + block.shape[0]] = block
                base += block.shape[0]

    def inside_mask(first, rows):
        pair = lax.broadcasted_iota(jnp.int32, (rows, 128), 0) // 16 + first + (32 * z - 8)
        return (pair >= 0) & (pair < 128)

    def row_copies(st, buf, chunk, lo, hi):
        rows = pl.ds(16 * lo, 16 * (hi - lo))
        copies = []
        for d, (to, slot, exists) in enumerate(((row + 1, 0, has_down), (row - 1, 2, has_up))):
            copies.append((exists, pltpu.make_async_remote_copy(
                src_ref=buf.at[1, rows], dst_ref=buf.at[slot, rows],
                send_sem=row_send.at[st, d, chunk], recv_sem=row_recv.at[st, d, chunk],
                device_id=holder(to), device_id_type=MESH,
            )))
        return copies

    def send_rows(st, buf, chunk, lo, hi):
        for exists, copy in row_copies(st, buf, chunk, lo, hi):
            pl.when(exists)(copy.start)

    def wait_sent(st, buf, chunk, lo, hi):
        for exists, copy in row_copies(st, buf, chunk, lo, hi):
            pl.when(exists)(copy.wait_send)

    def wait_rows(st, buf, chunk, lo, hi):
        rows = pl.ds(16 * lo, 16 * (hi - lo))
        for d, (slot, exists) in enumerate(((0, has_up), (2, has_down))):
            ref = buf.at[slot, rows]
            pl.when(exists)(pltpu.make_async_copy(ref, ref, row_recv.at[st, d, chunk]).wait)

    gain1 = vec_ref[0:1, :]
    off1 = vec_ref[1:2, :]
    gain2 = vec_ref[2:3, :]
    off2 = vec_ref[3:4, :]
    off3 = vec_ref[4:5, :]

    for g in range(4):
        ref = inb.at[g, pl.ds(0, 12 * WINDOW)]
        pltpu.make_async_copy(ref, ref, in_recv.at[g]).wait()

    def act1(i):
        first = 4 + 4 * i
        start = pl.multiple_of(48 * i + 48, 16)
        groups = [inb[g, pl.ds(start, 48), :].astype(F32) for g in range(4)]
        tiles = [
            jnp.concatenate([g[4 * k : 4 * k + 4] for g in groups], axis=0) for k in range(12)
        ]
        x = [jnp.concatenate(tiles[i3::3], axis=0) for i3 in range(3)]
        acts = pair_norm_silu(*x, gain1, inside_mask(first, 64))
        rows = pl.ds(pl.multiple_of(64 * i + 64, 64), 64)
        for n in range(3):
            xin[rows, 128 * n : 128 * (n + 1)] = x[n].astype(BF16)
            p1[1, rows, 128 * n : 128 * (n + 1)] = acts[n]

    done = 4
    for chunk in range(N):
        end = -(-ACT1[chunk + 1] // 4) * 4
        lax.fori_loop((done - 4) // 4, (end - 4) // 4, lambda i, c: (act1(i), c)[1], 0)
        done = end
        send_rows(0, p1, chunk, ACT1[chunk], ACT1[chunk + 1])

    def conv(buf, we, wo, lo, hi):
        m = 16 * (hi - lo)
        here, before, after = (pl.ds(16 * (lo + k), m) for k in (0, -1, 1))
        even, odd = [], []
        for q in range(3):
            even += [buf[q, here, :], buf[q, before, 128:384]]
            odd += [buf[q, here, :], buf[q, after, 0:256]]
        outs = []
        t = lax.broadcasted_iota(jnp.int32, (m, 192), 0) % 16
        for lhs, w in ((even, we), (odd, wo)):
            lhs = jnp.concatenate(lhs, axis=1)
            y = [jnp.dot(lhs, w[p].reshape(1920, 192), preferred_element_type=F32) for p in range(3)]
            total = y[2] + jnp.where(t >= 1, pltpu.roll(y[1], 1, 0), 0.0)
            total = total + jnp.where(t >= 2, pltpu.roll(y[0], 2, 0), 0.0)
            outs.append(total)
        e, o = outs
        blank = jnp.zeros((m, 64), F32)
        o = pltpu.roll(jnp.concatenate([o, blank], axis=1), 64, 1)
        e = jnp.concatenate([e, blank], axis=1)
        return [e[:, :128], e[:, 128:] + o[:, :128], o[:, 128:]]

    def conv1(chunk):
        lo, hi = CONV1[chunk], CONV1[chunk + 1]
        x = conv(p1, we1, wo1, lo, hi)
        x = [v + off1[:, 128 * n : 128 * (n + 1)] for n, v in enumerate(x)]
        acts = pair_norm_silu(*x, gain2, inside_mask(lo, 16 * (hi - lo)))
        for n in range(3):
            p2[1, 16 * lo : 16 * hi, 128 * n : 128 * (n + 1)] = acts[n]

    def conv2(chunk):
        lo, hi = CONV2[chunk], CONV2[chunk + 1]
        x = conv(p2, we2, wo2, lo, hi)
        inside = inside_mask(lo, 16 * (hi - lo))
        for n in range(3):
            lanes = slice(128 * n, 128 * (n + 1))
            v = xin[16 * lo : 16 * hi, lanes].astype(F32) + (x[n] + off2[:, lanes])
            p3[1, 16 * lo : 16 * hi, lanes] = jnp.where(inside, v, 0.0).astype(BF16)

    def upsample(chunk):
        lo, hi = UPS[chunk], UPS[chunk + 1]
        n = hi - lo
        m = 16 * n
        here, before, after = (pl.ds(16 * (lo + k), m) for k in (0, -1, 1))
        for a in range(2):
            even, odd = [], []
            for q in (a, a + 1):
                even += [p3[q, here, :], p3[q, before, 128:384]]
                odd += [p3[q, here, :], p3[q, after, 0:256]]
            e = jnp.dot(jnp.concatenate(even, axis=1), ue[a], preferred_element_type=F32)
            o = jnp.dot(jnp.concatenate(odd, axis=1), uo[a], preferred_element_type=F32)
            tiles = [e[:, :128], e[:, 128:] + o[:, :128], o[:, 128:]]
            for i3 in range(3):
                v = tiles[i3] + off3[:, 128 * i3 : 128 * (i3 + 1)]
                for j in range(n):
                    fbuf[pl.ds(16 * (6 * j + 2 * i3 + a), 16), :] = v[16 * j : 16 * j + 16]
        for t in range(16):
            v = fbuf[pl.ds(t, 6 * n, stride=16), :]
            stage[t, 6 * (lo - 8) : 6 * (hi - 8), :] = v.astype(BF16)

    def out_copies(chunk):
        lo, hi = 6 * (UPS[chunk] - 8), 6 * (UPS[chunk + 1] - 8)
        copies = []
        for g in range(4):
            src = stage.at[pl.ds(4 * g, 4), pl.ds(lo, hi - lo)]
            dst = out_ref.at[:, pl.ds(pl.multiple_of(192 * z + lo, 16), hi - lo)]
            local = pltpu.make_async_copy(src, dst, out_recv.at[chunk, z])
            remote = pltpu.make_async_remote_copy(
                src_ref=src, dst_ref=dst, send_sem=out_send.at[chunk, g], recv_sem=out_recv.at[chunk, z],
                device_id=(g, big * 2 + core), device_id_type=MESH,
            )
            copies.append(((tm == g) & (zl == core), local, remote))
        return copies

    for load in loads[:3]:
        load.wait()
    for chunk in range(N):
        wait_rows(0, p1, chunk, ACT1[chunk], ACT1[chunk + 1])
        conv1(chunk)
        send_rows(1, p2, chunk, CONV1[chunk], CONV1[chunk + 1])
    for load in loads[3:]:
        load.wait()
    for chunk in range(N):
        wait_rows(1, p2, chunk, CONV1[chunk], CONV1[chunk + 1])
        conv2(chunk)
        send_rows(2, p3, chunk, CONV2[chunk], CONV2[chunk + 1])
    for chunk in range(N):
        wait_rows(2, p3, chunk, CONV2[chunk], CONV2[chunk + 1])
        upsample(chunk)
        for mine, local, remote in out_copies(chunk):
            pl.when(mine)(local.start)
            pl.when(~mine)(remote.start)

    for zz in range(4):
        mine, local, remote = reshard(zz)
        pl.when(~mine)(remote.wait_send)
    for chunk in range(N):
        wait_sent(0, p1, chunk, ACT1[chunk], ACT1[chunk + 1])
        wait_sent(1, p2, chunk, CONV1[chunk], CONV1[chunk + 1])
        wait_sent(2, p3, chunk, CONV2[chunk], CONV2[chunk + 1])
    for chunk in range(N):
        for mine, local, remote in out_copies(chunk):
            pl.when(~mine)(remote.wait_send)
        for zz in range(4):
            lo, hi = 6 * (UPS[chunk] - 8), 6 * (UPS[chunk + 1] - 8)
            ref = out_ref.at[:, pl.ds(192 * zz + lo, hi - lo)]
            pltpu.make_async_copy(ref, ref, out_recv.at[chunk, zz]).wait()


def shards(features, gain1, kernel1, offset1, gain2, kernel2, offset2, up_kernel, up_offset):
    x = features.reshape(4, 384, 128).transpose(1, 0, 2).reshape(1536, 128)
    vec = jnp.stack(
        [jnp.tile(v, 2) for v in (gain1, offset1, gain2, offset2)] + [jnp.tile(up_offset, 4)] + [jnp.zeros(384)] * 3
    )
    dma = pltpu.SemaphoreType.DMA
    act = pltpu.VMEM((3, 16 * PAIRS, 384), BF16)
    weights = pltpu.VMEM((3, 3, 640, 192), BF16)
    out = pl.pallas_call(
        kernel,
        out_shape=jax.ShapeDtypeStruct((4, 768, 128), BF16),
        in_specs=[pl.BlockSpec(memory_space=pl.ANY)] * 3 + [pl.BlockSpec(memory_space=pltpu.VMEM)] * 2,
        out_specs=pl.BlockSpec(memory_space=pl.ANY),
        scratch_shapes=[
            pltpu.VMEM((4, 12 * PAIRS, 128), BF16),
            pltpu.VMEM((16 * PAIRS, 384), BF16),
            act, act, act,
            weights, weights, weights, weights,
            pltpu.VMEM((2, 1280, 256), BF16),
            pltpu.VMEM((2, 1280, 256), BF16),
            pltpu.VMEM((16 * 96, 128), F32),
            pltpu.VMEM((16, 192, 128), BF16),
            dma((4,)), dma((4,)),
            dma((3, 2, N)), dma((3, 2, N)),
            dma((N, 4)), dma((N, 4)),
            dma((6,)),
        ],
        compiler_params=pltpu.CompilerParams(
            collective_id=0, has_side_effects=True, vmem_limit_bytes=48 * 1024 * 1024
        ),
    )(x, kernel1.reshape(3, 3, 576, 192), kernel2.reshape(3, 3, 576, 192), up_kernel, vec)
    return out.reshape(4, 384, 2, 128).transpose(0, 2, 1, 3).reshape(4, 2, 49152)


def solution(mesh):
    placed = (P("tm", "tile", None), P(), P(), P(), P(), P(), P(), P(), P())
    return jax.shard_map(
        shards, mesh=mesh, in_specs=placed, out_specs=P("tm", "tile", None), check_vma=False
    )
```

time: 176 us -> 57.2 us (0.33)
  waiting for transfers between devices: 59 us -> 0 us
  Pallas kernels: 0 us -> 48.4 us
  starting transfers between devices: 44.2 us -> 0 us
  local copies, waits for them, and re-layouts: 34.7 us -> 8.47 us
  other arithmetic: 19.9 us -> 0 us
  matrix products: 16.8 us -> 0 us
    ppermute x8 -> x0, waiting for transfers between devices: 59 us -> none  [the longest x3 32.7 us: with_halo(): lax.ppermute(tail, axis, [(i, (i + 1) % count) for i in range(ends)])]
    pallas_call x0 -> x1, Pallas kernels: none -> 48.4 us  [shards(): pl.pallas_call(kernel, out_shape=jax.ShapeDtypeStruct((4, 768, 128), BF16...]
    ppermute x8 -> x0, starting transfers between devices: 44.2 us -> none  [the longest x3 19.1 us: with_halo(): lax.ppermute(head, axis, [((i + 1) % count, i) for i in range(ends)])]
    concatenate x8 -> x0, other arithmetic: 18.8 us -> none  [the longest x2 8.37 us: causal_conv(): jnp.concatenate([padded[:, :, shift_col:shift_col + columns, :] for shift...]
    slice x12 -> x0, local copies, waits for them, and re-layouts: 17.7 us -> none  [the longest x2 5.94 us: causal_conv(): kernel[temporal, vertical].reshape(3 * channels, outgoing)]
    dot_general x21 -> x0, matrix products: 16.8 us -> none  [the longest x18 11.5 us: causal_conv(): jnp.dot(window, kernel[temporal, vertical].reshape(3 * channels, outgoing...]
    ppermute x6 -> x0, local copies, waits for them, and re-layouts: 8.19 us -> none  [the longest x3 4.1 us: with_halo(): lax.ppermute(head, axis, [((i + 1) % count, i) for i in range(ends)])]
    unnamed x42 -> x7, local copies, waits for them, and re-layouts: 0.71 us -> 4.63 us
  transfers between devices with their start and end apart: 8 -> 0, of which waited for: 8 -> 0; matrix products, arithmetic and copies ran while one was open for 7% -> 0% of each run, Pallas kernels for 0% -> 0%
where the time goes in v1:
time: 57.2 us; the launch traced here: 56.9 us
  Pallas kernels  48.4 us (85%)
  local copies, waits for them, and re-layouts  8.47 us (15%)
    pallas_call x1, Pallas kernels, shards(): pl.pallas_call(kernel, out_shape=jax.ShapeDtypeStruct((4, 768, 128), BF16...  48.4 us
    unnamed x7, local copies, waits for them, and re-layouts  4.63 us
    another operation x4, local copies, waits for them, and re-layouts, shards(): jnp.tile(v, 2)  2.72 us

profile of v1, /device:TPU:7, one launch (start us, length us, event | category | flops | bytes accessed | tf_op | source)
XLA Modules:
  0.0 56.9 jit_solution(6308398705144256097)
XLA Ops:
  0.0 0.7 %tile.10 = f32[2,192]{1,0:T(2,128)S(1)} broadcast(f32[192]{0:T(256)} %param.10), dimensions={1} | broadcast | bytes 2304 | tf_op jit(solution)/shard_map/tile | solution.py:315
  0.7 0.1 stack_tile.15
  0.8 0.7 %tile.11 = f32[2,192]{1,0:T(2,128)S(1)} broadcast(f32[192]{0:T(256)} %param.12), dimensions={1} | broadcast | bytes 2304 | tf_op jit(solution)/shard_map/tile | solution.py:315
  1.4 0.1 stack_tile.16
  1.5 0.7 %tile.12 = f32[2,192]{1,0:T(2,128)S(1)} broadcast(f32[192]{0:T(256)} %param.13), dimensions={1} | broadcast | bytes 2304 | tf_op jit(solution)/shard_map/tile | solution.py:315
  2.2 0.1 stack_tile.17
  2.3 0.7 %tile.13 = f32[2,192]{1,0:T(2,128)S(1)} broadcast(f32[192]{0:T(256)} %param.15), dimensions={1} | broadcast | bytes 2304 | tf_op jit(solution)/shard_map/tile | solution.py:315
  3.0 0.1 stack_tile.18
  3.1 0.7 %tile.14 = f32[4,96]{1,0:T(4,128)S(1)} broadcast(f32[96]{0:T(128)} %param.17), dimensions={1} | broadcast | bytes 1920 | tf_op jit(solution)/shard_map/tile | solution.py:315
  3.7 0.1 stack_tile.19
  3.8 0.0 copy-start
  3.9 1.7 %copy-done = bf16[3,3,3,192,192]{4,3,2,1,0:T(8,128)(2,1)S(1)} copy-done((bf16[3,3,3,192,192]{4,3,2,1,0:T(8,128)(2,1)S(1)}, bf16[3,3,3,192,192]{4,3,2,1,0:T(8,128)(2,1)}, u32[]{:S(2)}) %copy-start) | copy-done | bytes 1990680
  5.6 0.0 copy-start.1
  5.6 1.0 %copy-done.1 = bf16[3,3,192,96]{3,2,1,0:T(8,128)(2,1)S(1)} copy-done((bf16[3,3,192,96]{3,2,1,0:T(8,128)(2,1)S(1)}, bf16[3,3,192,96]{3,2,1,0:T(8,128)(2,1)}, u32[]{:S(2)}) %copy-start.1) | copy-done | bytes 331800
  6.6 0.0 copy-start.2
  6.6 1.0 %copy-done.2 = bf16[4,1,49152]{2,0,1:T(4,128)(2,1)S(1)} copy-done((bf16[4,1,49152]{2,0,1:T(4,128)(2,1)S(1)}, bf16[4,1,49152]{2,0,1:T(4,128)(2,1)}, u32[]{:S(2)}) %copy-start.2) | copy-done | bytes 393240
  7.6 48.4 %shard_map.91 = bf16[4,768,128]{2,1,0:T(8,128)(2,1)S(1)} custom-call(bf16[1536,128]{1,0:T(8,128)(2,1)S(1)} %bitcast.14, bf16[3,3,576,192]{3,2,1,0:T(8,128)(2,1)S(1)} %bitcast.13, bf16[3,3,576,192]{3,2,1,0:T(8,128)(2,1)} %bitcast.15, bf16[3,3,192,96]{3,2,1,0:T(8,128)(2,1)S(1)} %copy-done.1, f32[8,384]{1,0:T(8,128)S(1)} %stack.7.vec_ref), custom_call_target="tpu_custom_call" | custom-call | tf_op jit(solution)/shard_map/pallas_call | solution.py:320
  56.0 0.9 %copy.13 = bf16[4,2,49152]{2,1,0:T(2,128)(2,1)} copy(bf16[4,2,49152]{2,1,0:T(2,128)(2,1)S(1)} %bitcast.12) | data formatting | bytes 1572864
  (3 shorter events, 0.0 us)
Async XLA Ops:
  3.8 1.8 %copy-start = (bf16[3,3,3,192,192]{4,3,2,1,0:T(8,128)(2,1)S(1)}, bf16[3,3,3,192,192]{4,3,2,1,0:T(8,128)(2,1)}, u32[]{:S(2)}) copy-start(bf16[3,3,3,192,192]{4,3,2,1,0:T(8,128)(2,1)} %param.11) | copy-start | bytes 5971972
  5.6 1.0 %copy-start.1 = (bf16[3,3,192,96]{3,2,1,0:T(8,128)(2,1)S(1)}, bf16[3,3,192,96]{3,2,1,0:T(8,128)(2,1)}, u32[]{:S(2)}) copy-start(bf16[3,3,192,96]{3,2,1,0:T(8,128)(2,1)} %uk_ref.1) | copy-start | bytes 995332
  6.6 1.0 %copy-start.2 = (bf16[4,1,49152]{2,0,1:T(4,128)(2,1)S(1)}, bf16[4,1,49152]{2,0,1:T(4,128)(2,1)}, u32[]{:S(2)}) copy-start(bf16[4,1,49152]{2,0,1:T(4,128)(2,1)} %param.9) | copy-start | bytes 1179652

commit v2 on v1

--- a/solution.py
+++ b/solution.py
@@ -39,8 +39,8 @@
 
 
 def kernel(
-    x_ref, w1_ref, w2_ref, uk_ref, vec_ref, out_ref,
-    inb, xin, p1, p2, p3, we1, wo1, we2, wo2, ue, uo, fbuf, stage,
+    x_ref, w1_ref, w2_ref, up_ref, g1_ref, o1_ref, g2_ref, o2_ref, o3_ref, out_ref,
+    inb, xin, p1, p2, p3, we1, wo1, we2, wo2, ue, uo, fbuf, stage, uk_ref, vg1, vo1, vg2, vo2, vo3,
     in_send, in_recv, row_send, row_recv, out_send, out_recv, w_sem,
 ):
     tm = lax.axis_index("tm")
@@ -81,7 +81,13 @@
         pltpu.make_async_copy(w2_ref.at[:, :, pl.ds(192, 384)], we2.at[:, :, pl.ds(0, 384)], w_sem.at[4]),
         pltpu.make_async_copy(w2_ref.at[:, :, pl.ds(0, 192)], we2.at[:, :, pl.ds(448, 192)], w_sem.at[5]),
     ]
-    for load in loads:
+    small = [
+        pltpu.make_async_copy(ref, to, w_sem.at[6 + i])
+        for i, (ref, to) in enumerate(
+            ((g1_ref, vg1), (o1_ref, vo1), (g2_ref, vg2), (o2_ref, vo2), (o3_ref, vo3))
+        )
+    ] + [pltpu.make_async_copy(up_ref, uk_ref, w_sem.at[11])]
+    for load in small + loads:
         load.start()
 
     pl.semaphore_wait(barrier, jnp.where(zl == core, 5, 6) + has_outer.astype(jnp.int32))
@@ -120,6 +126,8 @@
         for buf in (p1, p2, p3):
             buf[2] = jnp.zeros((16 * PAIRS, 384), BF16)
 
+    for load in small:
+        load.wait()
     src_lane = lax.broadcasted_iota(jnp.int32, (96, 256), 0)
     dst_lane = lax.broadcasted_iota(jnp.int32, (96, 256), 1)
     for u_ref, shift in ((ue, 0), (uo, 64)):
@@ -170,11 +178,20 @@
             ref = buf.at[slot, rows]
             pl.when(exists)(pltpu.make_async_copy(ref, ref, row_recv.at[st, d, chunk]).wait)
 
-    gain1 = vec_ref[0:1, :]
-    off1 = vec_ref[1:2, :]
-    gain2 = vec_ref[2:3, :]
-    off2 = vec_ref[3:4, :]
-    off3 = vec_ref[4:5, :]
+    lane8 = lax.broadcasted_iota(jnp.int32, (8, 128), 1)
+
+    def widened(ref):
+        v = jnp.concatenate([ref[...], jnp.zeros((1, 256 - ref.shape[1]), F32)], axis=1)
+        return jnp.broadcast_to(v, (8, 256))
+
+    def doubled(ref):
+        v = widened(ref)
+        r = pltpu.roll(v, 64, 1)
+        return jnp.concatenate([v[:, :128], jnp.where(lane8 < 64, v[:, 128:], r[:, :128]), r[:, 128:]], axis=1)[0:1]
+
+    gain1, off1, gain2, off2 = [doubled(ref) for ref in (vg1, vo1, vg2, vo2)]
+    quarter = jnp.concatenate([widened(vo3), jnp.zeros((8, 128), F32)], axis=1)
+    off3 = (quarter + pltpu.roll(quarter, 96, 1) + pltpu.roll(quarter, 192, 1) + pltpu.roll(quarter, 288, 1))[0:1]
 
     for g in range(4):
         ref = inb.at[g, pl.ds(0, 12 * WINDOW)]
@@ -311,16 +328,14 @@
 
 def shards(features, gain1, kernel1, offset1, gain2, kernel2, offset2, up_kernel, up_offset):
     x = features.reshape(4, 384, 128).transpose(1, 0, 2).reshape(1536, 128)
-    vec = jnp.stack(
-        [jnp.tile(v, 2) for v in (gain1, offset1, gain2, offset2)] + [jnp.tile(up_offset, 4)] + [jnp.zeros(384)] * 3
-    )
+    small = [v.reshape(1, -1) for v in (gain1, offset1, gain2, offset2, up_offset)]
     dma = pltpu.SemaphoreType.DMA
     act = pltpu.VMEM((3, 16 * PAIRS, 384), BF16)
     weights = pltpu.VMEM((3, 3, 640, 192), BF16)
     out = pl.pallas_call(
         kernel,
         out_shape=jax.ShapeDtypeStruct((4, 768, 128), BF16),
-        in_specs=[pl.BlockSpec(memory_space=pl.ANY)] * 3 + [pl.BlockSpec(memory_space=pltpu.VMEM)] * 2,
+        in_specs=[pl.BlockSpec(memory_space=pl.ANY)] * 9,
         out_specs=pl.BlockSpec(memory_space=pl.ANY),
         scratch_shapes=[
             pltpu.VMEM((4, 12 * PAIRS, 128), BF16),
@@ -331,15 +346,17 @@
             pltpu.VMEM((2, 1280, 256), BF16),
             pltpu.VMEM((16 * 96, 128), F32),
             pltpu.VMEM((16, 192, 128), BF16),
+            pltpu.VMEM((3, 3, 192, 96), BF16),
+            *[pltpu.VMEM((1, n), F32) for n in (192, 192, 192, 192, 96)],
             dma((4,)), dma((4,)),
             dma((3, 2, N)), dma((3, 2, N)),
             dma((N, 4)), dma((N, 4)),
-            dma((6,)),
+            dma((12,)),
         ],
         compiler_params=pltpu.CompilerParams(
-            collective_id=0, has_side_effects=True, vmem_limit_bytes=48 * 1024 * 1024
+            collective_id=0, has_side_effects=True, vmem_limit_bytes=60 * 1024 * 1024
         ),
-    )(x, kernel1.reshape(3, 3, 576, 192), kernel2.reshape(3, 3, 576, 192), up_kernel, vec)
+    )(x, kernel1.reshape(3, 3, 576, 192), kernel2.reshape(3, 3, 576, 192), up_kernel, *small)
     return out.reshape(4, 384, 2, 128).transpose(0, 2, 1, 3).reshape(4, 2, 49152)
 
 

time: 57.2 us -> 51.5 us (0.900)
  local copies, waits for them, and re-layouts: 8.47 us -> 2.55 us
    another operation x13 -> x0, local copies, waits for them, and re-layouts: 3.84 us -> none  [the longest x4 2.72 us: shards(): jnp.tile(v, 2)]
    unnamed x7 -> x1, local copies, waits for them, and re-layouts: 4.63 us -> 2.55 us
where the time goes in v2:
time: 51.5 us; the launch traced here: 51.4 us
  Pallas kernels  48.8 us (95%)
  local copies, waits for them, and re-layouts  2.55 us (5%)
    pallas_call x1, Pallas kernels, shards(): pl.pallas_call(kernel, out_shape=jax.ShapeDtypeStruct((4, 768, 128), BF16...  48.8 us
    unnamed x1, local copies, waits for them, and re-layouts  2.55 us

profile of v2, /device:TPU:7, one launch (start us, length us, event | category | flops | bytes accessed | tf_op | source)
XLA Modules:
  0.0 51.4 jit_solution(420246969871702433)
XLA Ops:
  0.0 48.8 %shard_map.91 = bf16[4,768,128]{2,1,0:T(8,128)(2,1)} custom-call(bf16[1536,128]{1,0:T(8,128)(2,1)} %bitcast.20, bf16[3,3,576,192]{3,2,1,0:T(8,128)(2,1)} %bitcast.18, bf16[3,3,576,192]{3,2,1,0:T(8,128)(2,1)} %bitcast.19, bf16[3,3,192,96]{3,2,1,0:T(8,128)(2,1)} %up_ref.1, f32[1,192]{1,0:T(1,128)} %bitcast.21, f32[1,192]{1,0:T(1,128)} %bitcast.22, ...), custom_call_target="tpu_custom_call" | custom-call | tf_op jit(solution)/shard_map/pallas_call | solution.py:335
  48.8 2.6 %copy.13 = bf16[4,2,49152]{2,1,0:T(2,128)(2,1)} copy(bf16[4,2,49152]{2,1,0:T(2,128)(2,1)} %bitcast.17) | data formatting | bytes 1572864

commit v3 on v2

--- a/solution.py
+++ b/solution.py
@@ -12,14 +12,15 @@
 F32 = jnp.float32
 BF16 = jnp.bfloat16
 PAIRS = 48
-ACT1 = (6, 28, 42)
-CONV1 = (7, 26, 41)
-CONV2 = (7, 25, 41)
-UPS = (8, 24, 40)
-N = len(UPS) - 1
-WINDOW = 40
-SRC_PAIR = (0, 28, 60, 88)
-DST_PAIR = (8, 4, 4, 0)
+INPUT = (4, 12, 20, 28, 36, 44)
+ACT1 = (6, *INPUT[1:-1], 42)
+CONV1 = (7, 11, 18, 26, 34, 41)
+CONV2 = (7, 10, 17, 25, 33, 41)
+UPS = (8, 16, 24, 32, 40)
+BOUNDS = (ACT1, CONV1, CONV2, UPS)
+COUNTS = tuple(len(b) - 1 for b in BOUNDS)
+MOST = max(COUNTS)
+ORDER = "00 01 02 03 10 04 11 12 13 20 14 21 22 23 24 30 31 32 33"
 
 
 def pair_norm_silu(x0, x1, x2, gain, inside):
@@ -40,7 +41,7 @@
 
 def kernel(
     x_ref, w1_ref, w2_ref, up_ref, g1_ref, o1_ref, g2_ref, o2_ref, o3_ref, out_ref,
-    inb, xin, p1, p2, p3, we1, wo1, we2, wo2, ue, uo, fbuf, stage, uk_ref, vg1, vo1, vg2, vo2, vo3,
+    inb, xin, p1, p2, p3, wb1, wb2, ue, uo, fbuf, stage, uk_ref, vg1, vo1, vg2, vo2, vo3,
     in_send, in_recv, row_send, row_recv, out_send, out_recv, w_sem,
 ):
     tm = lax.axis_index("tm")
@@ -74,44 +75,21 @@
         pl.semaphore_signal(barrier, inc=1, device_id=holder(outer), device_id_type=MESH)
 
     loads = [
-        pltpu.make_async_copy(w1_ref, wo1.at[:, :, pl.ds(0, 576)], w_sem.at[0]),
-        pltpu.make_async_copy(w1_ref.at[:, :, pl.ds(192, 384)], we1.at[:, :, pl.ds(0, 384)], w_sem.at[1]),
-        pltpu.make_async_copy(w1_ref.at[:, :, pl.ds(0, 192)], we1.at[:, :, pl.ds(448, 192)], w_sem.at[2]),
-        pltpu.make_async_copy(w2_ref, wo2.at[:, :, pl.ds(0, 576)], w_sem.at[3]),
-        pltpu.make_async_copy(w2_ref.at[:, :, pl.ds(192, 384)], we2.at[:, :, pl.ds(0, 384)], w_sem.at[4]),
-        pltpu.make_async_copy(w2_ref.at[:, :, pl.ds(0, 192)], we2.at[:, :, pl.ds(448, 192)], w_sem.at[5]),
+        pltpu.make_async_copy(ref, to.at[:, :, pl.ds(64, 576)], w_sem.at[i])
+        for i, (ref, to) in enumerate(((w1_ref, wb1), (w2_ref, wb2)))
     ]
     small = [
-        pltpu.make_async_copy(ref, to, w_sem.at[6 + i])
+        pltpu.make_async_copy(ref, to, w_sem.at[2 + i])
         for i, (ref, to) in enumerate(
             ((g1_ref, vg1), (o1_ref, vo1), (g2_ref, vg2), (o2_ref, vo2), (o3_ref, vo3))
         )
-    ] + [pltpu.make_async_copy(up_ref, uk_ref, w_sem.at[11])]
-    for load in small + loads:
+    ] + [pltpu.make_async_copy(up_ref, uk_ref, w_sem.at[7])]
+    for load in small:
         load.start()
 
-    pl.semaphore_wait(barrier, jnp.where(zl == core, 5, 6) + has_outer.astype(jnp.int32))
-
-    def reshard(zz):
-        src = x_ref.at[pl.ds(12 * SRC_PAIR[zz], 12 * WINDOW)]
-        dst = inb.at[tm, pl.ds(12 * DST_PAIR[zz], 12 * WINDOW)]
-        local = pltpu.make_async_copy(src, dst, in_recv.at[tm])
-        remote = pltpu.make_async_remote_copy(
-            src_ref=src, dst_ref=dst, send_sem=in_send.at[zz], recv_sem=in_recv.at[tm],
-            device_id=((zz // 2) * 2 + zl, big * 2 + zz % 2), device_id_type=MESH,
-        )
-        return (z == zz) & (zl == core), local, remote
-
-    for zz in range(4):
-        mine, local, remote = reshard(zz)
-        pl.when(mine)(local.start)
-        pl.when(~mine)(remote.start)
-
-    zeros64 = jnp.zeros((3, 3, 64, 192), BF16)
-    we1[:, :, 384:448] = zeros64
-    wo1[:, :, 576:640] = zeros64
-    we2[:, :, 384:448] = zeros64
-    wo2[:, :, 576:640] = zeros64
+    for buf in (wb1, wb2):
+        for base in (0, 640):
+            buf[:, :, base : base + 64] = jnp.zeros((3, 3, 64, 192), BF16)
     for buf in (p2, p3):
         for b in (6, 41):
             buf[:, 16 * b : 16 * b + 16] = jnp.zeros((3, 16, 384), BF16)
@@ -125,6 +103,56 @@
     def _():
         for buf in (p1, p2, p3):
             buf[2] = jnp.zeros((16 * PAIRS, 384), BF16)
+
+    pl.semaphore_wait(barrier, jnp.where(zl == core, 5, 6) + has_outer.astype(jnp.int32))
+
+    def windows(chunk):
+        lo, hi = INPUT[chunk], INPUT[chunk + 1]
+        if chunk == 0:
+            return ((lambda zz: zz == 0, 8, hi), (lambda zz: zz != 0, lo, hi))
+        if chunk == COUNTS[0] - 1:
+            return ((lambda zz: zz == 3, lo, 40), (lambda zz: zz != 3, lo, hi))
+        return ((lambda zz: zz >= 0, lo, hi),)
+
+    def reshard(chunk, ahead, lo, hi):
+        zz = (z + ahead) % 4
+        src = x_ref.at[pl.ds(pl.multiple_of(12 * (lo - 8 + 32 * zz), 16), 12 * (hi - lo))]
+        dst = inb.at[tm, pl.ds(12 * lo, 12 * (hi - lo))]
+        local = pltpu.make_async_copy(src, dst, in_recv.at[chunk, tm])
+        remote = pltpu.make_async_remote_copy(
+            src_ref=src, dst_ref=dst, send_sem=in_send.at[chunk, ahead], recv_sem=in_recv.at[chunk, tm],
+            device_id=((zz // 2) * 2 + zl, big * 2 + zz % 2), device_id_type=MESH,
+        )
+        return zz, local, remote
+
+    for chunk in range(COUNTS[0]):
+        for ahead in (2, 1, 3, 0):
+            for fits, lo, hi in windows(chunk):
+                zz, local, remote = reshard(chunk, ahead, lo, hi)
+                if ahead == 0:
+                    pl.when(fits(zz) & (zl == core))(local.start)
+                    pl.when(fits(zz) & (zl != core))(remote.start)
+                else:
+                    pl.when(fits(zz))(remote.start)
+
+    for load in loads:
+        load.start()
+
+    def wait_input(chunk):
+        for fits, lo, hi in windows(chunk):
+
+            @pl.when(fits(z))
+            def _():
+                for g in range(4):
+                    ref = inb.at[g, pl.ds(12 * lo, 12 * (hi - lo))]
+                    pltpu.make_async_copy(ref, ref, in_recv.at[chunk, g]).wait()
+
+    def wait_input_sent(chunk):
+        for ahead in range(4):
+            for fits, lo, hi in windows(chunk):
+                zz, local, remote = reshard(chunk, ahead, lo, hi)
+                go = fits(zz) if ahead else fits(zz) & (zl != core)
+                pl.when(go)(remote.wait_send)
 
     for load in small:
         load.wait()
@@ -153,8 +181,14 @@
         pair = lax.broadcasted_iota(jnp.int32, (rows, 128), 0) // 16 + first + (32 * z - 8)
         return (pair >= 0) & (pair < 128)
 
-    def row_copies(st, buf, chunk, lo, hi):
-        rows = pl.ds(16 * lo, 16 * (hi - lo))
+    bufs = (p1, p2, p3)
+
+    def chunk_rows(st, chunk):
+        lo, hi = BOUNDS[st][chunk], BOUNDS[st][chunk + 1]
+        return pl.ds(16 * lo, 16 * (hi - lo))
+
+    def row_copies(st, chunk):
+        buf, rows = bufs[st], chunk_rows(st, chunk)
         copies = []
         for d, (to, slot, exists) in enumerate(((row + 1, 0, has_down), (row - 1, 2, has_up))):
             copies.append((exists, pltpu.make_async_remote_copy(
@@ -164,19 +198,23 @@
             )))
         return copies
 
-    def send_rows(st, buf, chunk, lo, hi):
-        for exists, copy in row_copies(st, buf, chunk, lo, hi):
+    def send_rows(st, chunk):
+        for exists, copy in row_copies(st, chunk):
             pl.when(exists)(copy.start)
 
-    def wait_sent(st, buf, chunk, lo, hi):
-        for exists, copy in row_copies(st, buf, chunk, lo, hi):
+    def wait_sent(st, chunk):
+        for exists, copy in row_copies(st, chunk):
             pl.when(exists)(copy.wait_send)
 
-    def wait_rows(st, buf, chunk, lo, hi):
-        rows = pl.ds(16 * lo, 16 * (hi - lo))
-        for d, (slot, exists) in enumerate(((0, has_up), (2, has_down))):
-            ref = buf.at[slot, rows]
-            pl.when(exists)(pltpu.make_async_copy(ref, ref, row_recv.at[st, d, chunk]).wait)
+    waited = [0, 0, 0]
+
+    def wait_rows(st, end):
+        while waited[st] < COUNTS[st] and BOUNDS[st][waited[st]] < end:
+            chunk = waited[st]
+            for d, (slot, exists) in enumerate(((0, has_up), (2, has_down))):
+                ref = bufs[st].at[slot, chunk_rows(st, chunk)]
+                pl.when(exists)(pltpu.make_async_copy(ref, ref, row_recv.at[st, d, chunk]).wait)
+            waited[st] += 1
 
     lane8 = lax.broadcasted_iota(jnp.int32, (8, 128), 1)
 
@@ -193,43 +231,41 @@
     quarter = jnp.concatenate([widened(vo3), jnp.zeros((8, 128), F32)], axis=1)
     off3 = (quarter + pltpu.roll(quarter, 96, 1) + pltpu.roll(quarter, 192, 1) + pltpu.roll(quarter, 288, 1))[0:1]
 
-    for g in range(4):
-        ref = inb.at[g, pl.ds(0, 12 * WINDOW)]
-        pltpu.make_async_copy(ref, ref, in_recv.at[g]).wait()
-
-    def act1(i):
+    def act1_group(i):
         first = 4 + 4 * i
-        start = pl.multiple_of(48 * i + 48, 16)
+        start = 48 * i + 48
         groups = [inb[g, pl.ds(start, 48), :].astype(F32) for g in range(4)]
         tiles = [
             jnp.concatenate([g[4 * k : 4 * k + 4] for g in groups], axis=0) for k in range(12)
         ]
         x = [jnp.concatenate(tiles[i3::3], axis=0) for i3 in range(3)]
         acts = pair_norm_silu(*x, gain1, inside_mask(first, 64))
-        rows = pl.ds(pl.multiple_of(64 * i + 64, 64), 64)
+        rows = pl.ds(64 * i + 64, 64)
         for n in range(3):
             xin[rows, 128 * n : 128 * (n + 1)] = x[n].astype(BF16)
             p1[1, rows, 128 * n : 128 * (n + 1)] = acts[n]
 
-    done = 4
-    for chunk in range(N):
-        end = -(-ACT1[chunk + 1] // 4) * 4
-        lax.fori_loop((done - 4) // 4, (end - 4) // 4, lambda i, c: (act1(i), c)[1], 0)
-        done = end
-        send_rows(0, p1, chunk, ACT1[chunk], ACT1[chunk + 1])
-
-    def conv(buf, we, wo, lo, hi):
+    def act1(chunk):
+        wait_input(chunk)
+        for i in range(INPUT[chunk] // 4 - 1, INPUT[chunk + 1] // 4 - 1):
+            act1_group(i)
+        send_rows(0, chunk)
+
+    def conv(buf, wb, lo, hi):
         m = 16 * (hi - lo)
         here, before, after = (pl.ds(16 * (lo + k), m) for k in (0, -1, 1))
         even, odd = [], []
         for q in range(3):
-            even += [buf[q, here, :], buf[q, before, 128:384]]
+            even += [buf[q, before, 128:384], buf[q, here, :]]
             odd += [buf[q, here, :], buf[q, after, 0:256]]
         outs = []
         t = lax.broadcasted_iota(jnp.int32, (m, 192), 0) % 16
-        for lhs, w in ((even, we), (odd, wo)):
+        for lhs, base in ((even, 0), (odd, 64)):
             lhs = jnp.concatenate(lhs, axis=1)
-            y = [jnp.dot(lhs, w[p].reshape(1920, 192), preferred_element_type=F32) for p in range(3)]
+            y = [
+                jnp.dot(lhs, wb[p, :, base : base + 640].reshape(1920, 192), preferred_element_type=F32)
+                for p in range(3)
+            ]
             total = y[2] + jnp.where(t >= 1, pltpu.roll(y[1], 1, 0), 0.0)
             total = total + jnp.where(t >= 2, pltpu.roll(y[0], 2, 0), 0.0)
             outs.append(total)
@@ -240,24 +276,33 @@
         return [e[:, :128], e[:, 128:] + o[:, :128], o[:, 128:]]
 
     def conv1(chunk):
+        if chunk == 0:
+            loads[0].wait()
         lo, hi = CONV1[chunk], CONV1[chunk + 1]
-        x = conv(p1, we1, wo1, lo, hi)
+        wait_rows(0, hi + 1)
+        x = conv(p1, wb1, lo, hi)
         x = [v + off1[:, 128 * n : 128 * (n + 1)] for n, v in enumerate(x)]
         acts = pair_norm_silu(*x, gain2, inside_mask(lo, 16 * (hi - lo)))
         for n in range(3):
             p2[1, 16 * lo : 16 * hi, 128 * n : 128 * (n + 1)] = acts[n]
+        send_rows(1, chunk)
 
     def conv2(chunk):
+        if chunk == 0:
+            loads[1].wait()
         lo, hi = CONV2[chunk], CONV2[chunk + 1]
-        x = conv(p2, we2, wo2, lo, hi)
+        wait_rows(1, hi + 1)
+        x = conv(p2, wb2, lo, hi)
         inside = inside_mask(lo, 16 * (hi - lo))
         for n in range(3):
             lanes = slice(128 * n, 128 * (n + 1))
             v = xin[16 * lo : 16 * hi, lanes].astype(F32) + (x[n] + off2[:, lanes])
             p3[1, 16 * lo : 16 * hi, lanes] = jnp.where(inside, v, 0.0).astype(BF16)
+        send_rows(2, chunk)
 
     def upsample(chunk):
         lo, hi = UPS[chunk], UPS[chunk + 1]
+        wait_rows(2, hi + 1)
         n = hi - lo
         m = 16 * n
         here, before, after = (pl.ds(16 * (lo + k), m) for k in (0, -1, 1))
@@ -277,6 +322,10 @@
             v = fbuf[pl.ds(t, 6 * n, stride=16), :]
             stage[t, 6 * (lo - 8) : 6 * (hi - 8), :] = v.astype(BF16)
 
+        for mine, local, remote in out_copies(chunk):
+            pl.when(mine)(local.start)
+            pl.when(~mine)(remote.start)
+
     def out_copies(chunk):
         lo, hi = 6 * (UPS[chunk] - 8), 6 * (UPS[chunk + 1] - 8)
         copies = []
@@ -291,33 +340,15 @@
             copies.append(((tm == g) & (zl == core), local, remote))
         return copies
 
-    for load in loads[:3]:
-        load.wait()
-    for chunk in range(N):
-        wait_rows(0, p1, chunk, ACT1[chunk], ACT1[chunk + 1])
-        conv1(chunk)
-        send_rows(1, p2, chunk, CONV1[chunk], CONV1[chunk + 1])
-    for load in loads[3:]:
-        load.wait()
-    for chunk in range(N):
-        wait_rows(1, p2, chunk, CONV1[chunk], CONV1[chunk + 1])
-        conv2(chunk)
-        send_rows(2, p3, chunk, CONV2[chunk], CONV2[chunk + 1])
-    for chunk in range(N):
-        wait_rows(2, p3, chunk, CONV2[chunk], CONV2[chunk + 1])
-        upsample(chunk)
-        for mine, local, remote in out_copies(chunk):
-            pl.when(mine)(local.start)
-            pl.when(~mine)(remote.start)
-
-    for zz in range(4):
-        mine, local, remote = reshard(zz)
-        pl.when(~mine)(remote.wait_send)
-    for chunk in range(N):
-        wait_sent(0, p1, chunk, ACT1[chunk], ACT1[chunk + 1])
-        wait_sent(1, p2, chunk, CONV1[chunk], CONV1[chunk + 1])
-        wait_sent(2, p3, chunk, CONV2[chunk], CONV2[chunk + 1])
-    for chunk in range(N):
+    for stage_chunk in ORDER.split():
+        (act1, conv1, conv2, upsample)[int(stage_chunk[0])](int(stage_chunk[1]))
+
+    for chunk in range(COUNTS[0]):
+        wait_input_sent(chunk)
+    for st in range(3):
+        for chunk in range(COUNTS[st]):
+            wait_sent(st, chunk)
+    for chunk in range(COUNTS[3]):
         for mine, local, remote in out_copies(chunk):
             pl.when(~mine)(remote.wait_send)
         for zz in range(4):
@@ -331,30 +362,30 @@
     small = [v.reshape(1, -1) for v in (gain1, offset1, gain2, offset2, up_offset)]
     dma = pltpu.SemaphoreType.DMA
     act = pltpu.VMEM((3, 16 * PAIRS, 384), BF16)
-    weights = pltpu.VMEM((3, 3, 640, 192), BF16)
+    weights = pltpu.VMEM((3, 3, 704, 192), BF16)
     out = pl.pallas_call(
         kernel,
-        out_shape=jax.ShapeDtypeStruct((4, 768, 128), BF16),
+        out_shape=pltpu.VMEM((4, 768, 128), BF16),
         in_specs=[pl.BlockSpec(memory_space=pl.ANY)] * 9,
         out_specs=pl.BlockSpec(memory_space=pl.ANY),
         scratch_shapes=[
             pltpu.VMEM((4, 12 * PAIRS, 128), BF16),
             pltpu.VMEM((16 * PAIRS, 384), BF16),
             act, act, act,
-            weights, weights, weights, weights,
+            weights, weights,
             pltpu.VMEM((2, 1280, 256), BF16),
             pltpu.VMEM((2, 1280, 256), BF16),
             pltpu.VMEM((16 * 96, 128), F32),
             pltpu.VMEM((16, 192, 128), BF16),
             pltpu.VMEM((3, 3, 192, 96), BF16),
             *[pltpu.VMEM((1, n), F32) for n in (192, 192, 192, 192, 96)],
-            dma((4,)), dma((4,)),
-            dma((3, 2, N)), dma((3, 2, N)),
-            dma((N, 4)), dma((N, 4)),
-            dma((12,)),
+            dma((COUNTS[0], 4)), dma((COUNTS[0], 4)),
+            dma((3, 2, MOST)), dma((3, 2, MOST)),
+            dma((COUNTS[3], 4)), dma((COUNTS[3], 4)),
+            dma((8,)),
         ],
         compiler_params=pltpu.CompilerParams(
-            collective_id=0, has_side_effects=True, vmem_limit_bytes=60 * 1024 * 1024
+            collective_id=0, has_side_effects=True, vmem_limit_bytes=56 * 1024 * 1024
         ),
     )(x, kernel1.reshape(3, 3, 576, 192), kernel2.reshape(3, 3, 576, 192), up_kernel, *small)
     return out.reshape(4, 384, 2, 128).transpose(0, 2, 1, 3).reshape(4, 2, 49152)

time: 51.5 us -> 39.9 us (0.77)
  Pallas kernels: 48.8 us -> 38.9 us
  local copies, waits for them, and re-layouts: 2.55 us -> 0.88 us
    pallas_call x1, Pallas kernels: 48.8 us -> 38.9 us  [shards(): pl.pallas_call(kernel, out_shape=pltpu.VMEM((4, 768, 128), BF16), in_spec...]
    unnamed x1, local copies, waits for them, and re-layouts: 2.55 us -> 0.88 us
where the time goes in v3:
time: 39.9 us; the launch traced here: 39.8 us
  Pallas kernels  38.9 us (97%)
  local copies, waits for them, and re-layouts  0.88 us (2%)
    pallas_call x1, Pallas kernels, shards(): pl.pallas_call(kernel, out_shape=pltpu.VMEM((4, 768, 128), BF16), in_spec...  38.9 us
    unnamed x1, local copies, waits for them, and re-layouts  0.88 us

profile of v3, /device:TPU:7, one launch (start us, length us, event | category | flops | bytes accessed | tf_op | source)
XLA Modules:
  0.0 39.8 jit_solution(15898969880339011942)
XLA Ops:
  0.0 38.9 %shard_map.91 = bf16[4,768,128]{2,1,0:T(8,128)(2,1)S(1)} custom-call(bf16[1536,128]{1,0:T(8,128)(2,1)} %bitcast.20, bf16[3,3,576,192]{3,2,1,0:T(8,128)(2,1)} %bitcast.18, bf16[3,3,576,192]{3,2,1,0:T(8,128)(2,1)} %bitcast.19, bf16[3,3,192,96]{3,2,1,0:T(8,128)(2,1)} %up_ref.1, f32[1,192]{1,0:T(1,128)} %bitcast.21, f32[1,192]{1,0:T(1,128)} %bitcast.22, ...), custom_call_target="tpu_custom_call" | custom-call | tf_op jit(solution)/shard_map/pallas_call | solution.py:366
  38.9 0.9 %copy.13 = bf16[4,2,49152]{2,1,0:T(2,128)(2,1)} copy(bf16[4,2,49152]{2,1,0:T(2,128)(2,1)S(1)} %bitcast.17) | data formatting | bytes 1572864

commit v4 on v3

--- a/solution.py
+++ b/solution.py
@@ -14,13 +14,14 @@
 PAIRS = 48
 INPUT = (4, 12, 20, 28, 36, 44)
 ACT1 = (6, *INPUT[1:-1], 42)
-CONV1 = (7, 11, 18, 26, 34, 41)
-CONV2 = (7, 10, 17, 25, 33, 41)
+CONV1 = (7, 18, 26, 34, 41)
+CONV2 = (7, 17, 25, 33, 41)
 UPS = (8, 16, 24, 32, 40)
 BOUNDS = (ACT1, CONV1, CONV2, UPS)
 COUNTS = tuple(len(b) - 1 for b in BOUNDS)
 MOST = max(COUNTS)
-ORDER = "00 01 02 03 10 04 11 12 13 20 14 21 22 23 24 30 31 32 33"
+OUT_ROWS = tuple(16 * (3 * (b - 8) // 16) for b in UPS)
+ORDER = "00 01 02 03 04 10 11 12 13 20 21 30 22 31 23 32 40 41 42 33 43 50 51 52 53"
 
 
 def pair_norm_silu(x0, x1, x2, gain, inside):
@@ -41,7 +42,7 @@
 
 def kernel(
     x_ref, w1_ref, w2_ref, up_ref, g1_ref, o1_ref, g2_ref, o2_ref, o3_ref, out_ref,
-    inb, xin, p1, p2, p3, wb1, wb2, ue, uo, fbuf, stage, uk_ref, vg1, vo1, vg2, vo2, vo3,
+    inb, xin, p1, p2, p3, wb1, wb2, ue, uo, fbuf, stage, recvb, mixed, uk_ref, vg1, vo1, vg2, vo2, vo3,
     in_send, in_recv, row_send, row_recv, out_send, out_recv, w_sem,
 ):
     tm = lax.axis_index("tm")
@@ -118,9 +119,9 @@
         zz = (z + ahead) % 4
         src = x_ref.at[pl.ds(pl.multiple_of(12 * (lo - 8 + 32 * zz), 16), 12 * (hi - lo))]
         dst = inb.at[tm, pl.ds(12 * lo, 12 * (hi - lo))]
-        local = pltpu.make_async_copy(src, dst, in_recv.at[chunk, tm])
+        local = pltpu.make_async_copy(src, dst, in_recv.at[chunk])
         remote = pltpu.make_async_remote_copy(
-            src_ref=src, dst_ref=dst, send_sem=in_send.at[chunk, ahead], recv_sem=in_recv.at[chunk, tm],
+            src_ref=src, dst_ref=dst, send_sem=in_send.at[ahead], recv_sem=in_recv.at[chunk],
             device_id=((zz // 2) * 2 + zl, big * 2 + zz % 2), device_id_type=MESH,
         )
         return zz, local, remote
@@ -141,18 +142,15 @@
     def wait_input(chunk):
         for fits, lo, hi in windows(chunk):
 
-            @pl.when(fits(z))
-            def _():
-                for g in range(4):
-                    ref = inb.at[g, pl.ds(12 * lo, 12 * (hi - lo))]
-                    pltpu.make_async_copy(ref, ref, in_recv.at[chunk, g]).wait()
-
-    def wait_input_sent(chunk):
-        for ahead in range(4):
-            for fits, lo, hi in windows(chunk):
-                zz, local, remote = reshard(chunk, ahead, lo, hi)
-                go = fits(zz) if ahead else fits(zz) & (zl != core)
-                pl.when(go)(remote.wait_send)
+            ref = inb.at[:, pl.ds(12 * lo, 12 * (hi - lo))]
+            pl.when(fits(z))(pltpu.make_async_copy(ref, ref, in_recv.at[chunk]).wait)
+
+    def wait_input_sent(ahead):
+        zz = (z + ahead) % 4
+        for edge, pairs in (((zz == 0) | (zz == 3), 36), ((zz == 1) | (zz == 2), 40)):
+            ref = x_ref.at[pl.ds(0, 12 * pairs)]
+            go = edge if ahead else edge & (zl != core)
+            pl.when(go)(pltpu.make_async_copy(ref, ref, in_send.at[ahead]).wait)
 
     for load in small:
         load.wait()
@@ -183,8 +181,8 @@
 
     bufs = (p1, p2, p3)
 
-    def chunk_rows(st, chunk):
-        lo, hi = BOUNDS[st][chunk], BOUNDS[st][chunk + 1]
+    def chunk_rows(st, chunk, end=None):
+        lo, hi = BOUNDS[st][chunk], BOUNDS[st][chunk + 1 if end is None else end]
         return pl.ds(16 * lo, 16 * (hi - lo))
 
     def row_copies(st, chunk):
@@ -193,7 +191,7 @@
         for d, (to, slot, exists) in enumerate(((row + 1, 0, has_down), (row - 1, 2, has_up))):
             copies.append((exists, pltpu.make_async_remote_copy(
                 src_ref=buf.at[1, rows], dst_ref=buf.at[slot, rows],
-                send_sem=row_send.at[st, d, chunk], recv_sem=row_recv.at[st, d, chunk],
+                send_sem=row_send.at[st, d], recv_sem=row_recv.at[st, d, chunk],
                 device_id=holder(to), device_id_type=MESH,
             )))
         return copies
@@ -202,19 +200,22 @@
         for exists, copy in row_copies(st, chunk):
             pl.when(exists)(copy.start)
 
-    def wait_sent(st, chunk):
-        for exists, copy in row_copies(st, chunk):
-            pl.when(exists)(copy.wait_send)
-
-    waited = [0, 0, 0]
-
-    def wait_rows(st, end):
-        while waited[st] < COUNTS[st] and BOUNDS[st][waited[st]] < end:
-            chunk = waited[st]
-            for d, (slot, exists) in enumerate(((0, has_up), (2, has_down))):
-                ref = bufs[st].at[slot, chunk_rows(st, chunk)]
-                pl.when(exists)(pltpu.make_async_copy(ref, ref, row_recv.at[st, d, chunk]).wait)
-            waited[st] += 1
+    def wait_sent(st):
+        ref = bufs[st].at[1, chunk_rows(st, 0, -1)]
+        for d, exists in enumerate((has_down, has_up)):
+            pl.when(exists)(pltpu.make_async_copy(ref, ref, row_send.at[st, d]).wait)
+
+    waited = [[0, 0, 0], [0, 0, 0]]
+
+    def wait_rows(st, end, near):
+        seen = waited[near]
+        while seen[st] < COUNTS[st] and BOUNDS[st][seen[st]] < end:
+            chunk = seen[st]
+            d = 1 - core if near else core
+            ref = bufs[st].at[2 * d, chunk_rows(st, chunk)]
+            wait = pltpu.make_async_copy(ref, ref, row_recv.at[st, d, chunk]).wait
+            wait() if near else pl.when(has_outer)(wait)
+            seen[st] += 1
 
     lane8 = lax.broadcasted_iota(jnp.int32, (8, 128), 1)
 
@@ -279,7 +280,8 @@
         if chunk == 0:
             loads[0].wait()
         lo, hi = CONV1[chunk], CONV1[chunk + 1]
-        wait_rows(0, hi + 1)
+        wait_rows(0, hi + 1, True)
+        wait_rows(0, hi + 1, False)
         x = conv(p1, wb1, lo, hi)
         x = [v + off1[:, 128 * n : 128 * (n + 1)] for n, v in enumerate(x)]
         acts = pair_norm_silu(*x, gain2, inside_mask(lo, 16 * (hi - lo)))
@@ -291,7 +293,8 @@
         if chunk == 0:
             loads[1].wait()
         lo, hi = CONV2[chunk], CONV2[chunk + 1]
-        wait_rows(1, hi + 1)
+        wait_rows(1, hi + 1, True)
+        wait_rows(1, hi + 1, False)
         x = conv(p2, wb2, lo, hi)
         inside = inside_mask(lo, 16 * (hi - lo))
         for n in range(3):
@@ -300,61 +303,65 @@
             p3[1, 16 * lo : 16 * hi, lanes] = jnp.where(inside, v, 0.0).astype(BF16)
         send_rows(2, chunk)
 
-    def upsample(chunk):
+    def upsample(chunk, half):
         lo, hi = UPS[chunk], UPS[chunk + 1]
-        wait_rows(2, hi + 1)
-        n = hi - lo
-        m = 16 * n
+        wait_rows(2, hi + 1, half == 0)
+        phase = core if half else 1 - core
+        m = 16 * (hi - lo)
         here, before, after = (pl.ds(16 * (lo + k), m) for k in (0, -1, 1))
-        for a in range(2):
-            even, odd = [], []
-            for q in (a, a + 1):
-                even += [p3[q, here, :], p3[q, before, 128:384]]
-                odd += [p3[q, here, :], p3[q, after, 0:256]]
-            e = jnp.dot(jnp.concatenate(even, axis=1), ue[a], preferred_element_type=F32)
-            o = jnp.dot(jnp.concatenate(odd, axis=1), uo[a], preferred_element_type=F32)
-            tiles = [e[:, :128], e[:, 128:] + o[:, :128], o[:, 128:]]
-            for i3 in range(3):
-                v = tiles[i3] + off3[:, 128 * i3 : 128 * (i3 + 1)]
-                for j in range(n):
-                    fbuf[pl.ds(16 * (6 * j + 2 * i3 + a), 16), :] = v[16 * j : 16 * j + 16]
+        even, odd = [], []
+        for q in (phase, phase + 1):
+            even += [p3[q, here, :], p3[q, before, 128:384]]
+            odd += [p3[q, here, :], p3[q, after, 0:256]]
+        e = jnp.dot(jnp.concatenate(even, axis=1), ue[phase], preferred_element_type=F32)
+        o = jnp.dot(jnp.concatenate(odd, axis=1), uo[phase], preferred_element_type=F32)
+        tiles = [e[:, :128], e[:, 128:] + o[:, :128], o[:, 128:]]
+        for i3 in range(3):
+            v = tiles[i3] + off3[:, 128 * i3 : 128 * (i3 + 1)]
+            for j in range(lo, hi):
+                at = 16 * (3 * (j - 8) + i3)
+                fbuf[half, at : at + 16, :] = v[16 * (j - lo) : 16 * (j - lo) + 16]
+        first, last = OUT_ROWS[chunk], OUT_ROWS[chunk + 1]
         for t in range(16):
-            v = fbuf[pl.ds(t, 6 * n, stride=16), :]
-            stage[t, 6 * (lo - 8) : 6 * (hi - 8), :] = v.astype(BF16)
-
-        for mine, local, remote in out_copies(chunk):
-            pl.when(mine)(local.start)
-            pl.when(~mine)(remote.start)
-
-    def out_copies(chunk):
-        lo, hi = 6 * (UPS[chunk] - 8), 6 * (UPS[chunk + 1] - 8)
-        copies = []
+            v = fbuf[half, pl.ds(16 * first + t, last - first, stride=16), :]
+            stage[half, t, first:last, :] = v.astype(BF16)
         for g in range(4):
-            src = stage.at[pl.ds(4 * g, 4), pl.ds(lo, hi - lo)]
-            dst = out_ref.at[:, pl.ds(pl.multiple_of(192 * z + lo, 16), hi - lo)]
-            local = pltpu.make_async_copy(src, dst, out_recv.at[chunk, z])
-            remote = pltpu.make_async_remote_copy(
-                src_ref=src, dst_ref=dst, send_sem=out_send.at[chunk, g], recv_sem=out_recv.at[chunk, z],
+            src = stage.at[half, pl.ds(4 * g, 4), pl.ds(first, last - first)]
+            dst = recvb.at[half, z, :, pl.ds(first, last - first)]
+            mine = (tm == g) & (zl == core)
+            pl.when(mine)(pltpu.make_async_copy(src, dst, out_recv.at[half, chunk]).start)
+            pl.when(~mine)(pltpu.make_async_remote_copy(
+                src_ref=src, dst_ref=dst, send_sem=out_send.at[half, g], recv_sem=out_recv.at[half, chunk],
                 device_id=(g, big * 2 + core), device_id_type=MESH,
-            )
-            copies.append(((tm == g) & (zl == core), local, remote))
-        return copies
-
+            ).start)
+
+    def interleave(chunk):
+        first, last = OUT_ROWS[chunk], OUT_ROWS[chunk + 1]
+        n = last - first
+        for half in range(2):
+            ref = recvb.at[half, :, :, pl.ds(first, n)]
+            pltpu.make_async_copy(ref, ref, out_recv.at[half, chunk]).wait()
+        for zz in range(4):
+            for f in range(4):
+                at = 192 * (4 * zz + f)
+                for a in range(2):
+                    half = zl if a else 1 - zl
+                    mixed[pl.ds(at + a, n, stride=2), :] = recvb[half, zz, f, first:last, :].astype(F32)
+                out_ref[f, 192 * zz + 2 * first : 192 * zz + 2 * last, :] = mixed[at : at + 2 * n, :].astype(BF16)
+
+    work = (act1, conv1, conv2, lambda c: upsample(c, 0), lambda c: upsample(c, 1), interleave)
     for stage_chunk in ORDER.split():
-        (act1, conv1, conv2, upsample)[int(stage_chunk[0])](int(stage_chunk[1]))
-
-    for chunk in range(COUNTS[0]):
-        wait_input_sent(chunk)
+        work[int(stage_chunk[0])](int(stage_chunk[1]))
+
+    for ahead in range(4):
+        wait_input_sent(ahead)
     for st in range(3):
-        for chunk in range(COUNTS[st]):
-            wait_sent(st, chunk)
-    for chunk in range(COUNTS[3]):
-        for mine, local, remote in out_copies(chunk):
-            pl.when(~mine)(remote.wait_send)
-        for zz in range(4):
-            lo, hi = 6 * (UPS[chunk] - 8), 6 * (UPS[chunk + 1] - 8)
-            ref = out_ref.at[:, pl.ds(192 * zz + lo, hi - lo)]
-            pltpu.make_async_copy(ref, ref, out_recv.at[chunk, zz]).wait()
+        wait_sent(st)
+    for half in range(2):
+        for g in range(4):
+            ref = stage.at[half, pl.ds(4 * g, 4)]
+            mine = (tm == g) & (zl == core)
+            pl.when(~mine)(pltpu.make_async_copy(ref, ref, out_send.at[half, g]).wait)
 
 
 def shards(features, gain1, kernel1, offset1, gain2, kernel2, offset2, up_kernel, up_offset):
@@ -367,7 +374,7 @@
         kernel,
         out_shape=pltpu.VMEM((4, 768, 128), BF16),
         in_specs=[pl.BlockSpec(memory_space=pl.ANY)] * 9,
-        out_specs=pl.BlockSpec(memory_space=pl.ANY),
+        out_specs=pl.BlockSpec(memory_space=pltpu.VMEM),
         scratch_shapes=[
             pltpu.VMEM((4, 12 * PAIRS, 128), BF16),
             pltpu.VMEM((16 * PAIRS, 384), BF16),
@@ -375,13 +382,15 @@
             weights, weights,
             pltpu.VMEM((2, 1280, 256), BF16),
             pltpu.VMEM((2, 1280, 256), BF16),
-            pltpu.VMEM((16 * 96, 128), F32),
-            pltpu.VMEM((16, 192, 128), BF16),
+            pltpu.VMEM((2, 16 * 96, 128), F32),
+            pltpu.VMEM((2, 16, 96, 128), BF16),
+            pltpu.VMEM((2, 4, 4, 96, 128), BF16),
+            pltpu.VMEM((16 * 192, 128), F32),
             pltpu.VMEM((3, 3, 192, 96), BF16),
             *[pltpu.VMEM((1, n), F32) for n in (192, 192, 192, 192, 96)],
-            dma((COUNTS[0], 4)), dma((COUNTS[0], 4)),
-            dma((3, 2, MOST)), dma((3, 2, MOST)),
-            dma((COUNTS[3], 4)), dma((COUNTS[3], 4)),
+            dma((4,)), dma((COUNTS[0],)),
+            dma((3, 2)), dma((3, 2, MOST)),
+            dma((2, 4)), dma((2, COUNTS[3])),
             dma((8,)),
         ],
         compiler_params=pltpu.CompilerParams(

time: 39.9 us -> 37.1 us (0.930)
  Pallas kernels: 38.9 us -> 36.1 us
    pallas_call x1, Pallas kernels: 38.9 us -> 36.1 us  [shards(): pl.pallas_call(kernel, out_shape=pltpu.VMEM((4, 768, 128), BF16), in_spec...]
where the time goes in v4:
time: 37.1 us; the launch traced here: 37 us
  Pallas kernels  36.1 us (97%)
  local copies, waits for them, and re-layouts  0.88 us (2%)
    pallas_call x1, Pallas kernels, shards(): pl.pallas_call(kernel, out_shape=pltpu.VMEM((4, 768, 128), BF16), in_spec...  36.1 us
    unnamed x1, local copies, waits for them, and re-layouts  0.88 us

profile of v4, /device:TPU:7, one launch (start us, length us, event | category | flops | bytes accessed | tf_op | source)
XLA Modules:
  0.0 37.0 jit_solution(14112833107588880796)
XLA Ops:
  0.0 36.1 %shard_map.91 = bf16[4,768,128]{2,1,0:T(8,128)(2,1)S(1)} custom-call(bf16[1536,128]{1,0:T(8,128)(2,1)} %bitcast.20, bf16[3,3,576,192]{3,2,1,0:T(8,128)(2,1)} %bitcast.18, bf16[3,3,576,192]{3,2,1,0:T(8,128)(2,1)} %bitcast.19, bf16[3,3,192,96]{3,2,1,0:T(8,128)(2,1)} %up_ref.1, f32[1,192]{1,0:T(1,128)} %bitcast.21, f32[1,192]{1,0:T(1,128)} %bitcast.22, ...), custom_call_target="tpu_custom_call" | custom-call | tf_op jit(solution)/shard_map/pallas_call | solution.py:373
  36.1 0.9 %copy.13 = bf16[4,2,49152]{2,1,0:T(2,128)(2,1)} copy(bf16[4,2,49152]{2,1,0:T(2,128)(2,1)S(1)} %bitcast.17) | data formatting | bytes 1572864

commit v5 on v4

--- a/solution.py
+++ b/solution.py
@@ -21,7 +21,9 @@
 COUNTS = tuple(len(b) - 1 for b in BOUNDS)
 MOST = max(COUNTS)
 OUT_ROWS = tuple(16 * (3 * (b - 8) // 16) for b in UPS)
-ORDER = "00 01 02 03 04 10 11 12 13 20 21 30 22 31 23 32 40 41 42 33 43 50 51 52 53"
+ORDER = (
+    "00 01 02 10 03 11 04 12 20 21 13 22 30 23 31 40 32 41 50 42 51 33 52 43 60 61 62 53 63 70 71 72 73"
+)
 
 
 def pair_norm_silu(x0, x1, x2, gain, inside):
@@ -35,14 +37,14 @@
     outs = []
     for i, (x, s) in enumerate(zip((x0, x1, x2), scales)):
         v = x * s * gain[:, 128 * i : 128 * (i + 1)]
-        v = v / (1.0 + jnp.exp(-v))
-        outs.append(jnp.where(inside, v, 0.0).astype(BF16))
+        v = 0.5 * v * (1.0 + jnp.tanh(0.5 * v))
+        outs.append(inside(v).astype(BF16))
     return outs
 
 
 def kernel(
     x_ref, w1_ref, w2_ref, up_ref, g1_ref, o1_ref, g2_ref, o2_ref, o3_ref, out_ref,
-    inb, xin, p1, p2, p3, wb1, wb2, ue, uo, fbuf, stage, recvb, mixed, uk_ref, vg1, vo1, vg2, vo2, vo3,
+    inb, xin, p1, p2, p3, wb1, wb2, ue, uo, acc, fbuf, stage, recvb, mixed, uk_ref, vg1, vo1, vg2, vo2, vo3,
     in_send, in_recv, row_send, row_recv, out_send, out_recv, w_sem,
 ):
     tm = lax.axis_index("tm")
@@ -176,8 +178,10 @@
                 base += block.shape[0]
 
     def inside_mask(first, rows):
+        if first >= 8 and first + rows // 16 <= 40:
+            return lambda v: v
         pair = lax.broadcasted_iota(jnp.int32, (rows, 128), 0) // 16 + first + (32 * z - 8)
-        return (pair >= 0) & (pair < 128)
+        return lambda v: jnp.where((pair >= 0) & (pair < 128), v, 0.0)
 
     bufs = (p1, p2, p3)
 
@@ -252,21 +256,21 @@
             act1_group(i)
         send_rows(0, chunk)
 
-    def conv(buf, wb, lo, hi):
+    def conv(buf, wb, lo, hi, taps):
         m = 16 * (hi - lo)
         here, before, after = (pl.ds(16 * (lo + k), m) for k in (0, -1, 1))
         even, odd = [], []
-        for q in range(3):
+        for q in taps:
             even += [buf[q, before, 128:384], buf[q, here, :]]
             odd += [buf[q, here, :], buf[q, after, 0:256]]
         outs = []
         t = lax.broadcasted_iota(jnp.int32, (m, 192), 0) % 16
         for lhs, base in ((even, 0), (odd, 64)):
             lhs = jnp.concatenate(lhs, axis=1)
-            y = [
-                jnp.dot(lhs, wb[p, :, base : base + 640].reshape(1920, 192), preferred_element_type=F32)
-                for p in range(3)
-            ]
+            y = []
+            for p in range(3):
+                w = jnp.concatenate([wb[p, q, base : base + 640] for q in taps], axis=0)
+                y.append(jnp.dot(lhs, w, preferred_element_type=F32))
             total = y[2] + jnp.where(t >= 1, pltpu.roll(y[1], 1, 0), 0.0)
             total = total + jnp.where(t >= 2, pltpu.roll(y[0], 2, 0), 0.0)
             outs.append(total)
@@ -276,31 +280,44 @@
         e = jnp.concatenate([e, blank], axis=1)
         return [e[:, :128], e[:, 128:] + o[:, :128], o[:, 128:]]
 
-    def conv1(chunk):
+    def conv_near(st, chunk):
         if chunk == 0:
-            loads[0].wait()
+            loads[st].wait()
+        lo, hi = BOUNDS[st + 1][chunk], BOUNDS[st + 1][chunk + 1]
+        wait_rows(st, hi + 1, True)
+        x = conv(bufs[st], (wb1, wb2)[st], lo, hi, (1, 2 - 2 * core))
+        for n in range(3):
+            acc[st, 16 * lo : 16 * hi, 128 * n : 128 * (n + 1)] = x[n]
+
+    def conv_far(st, chunk, whole):
+        lo, hi = BOUNDS[st + 1][chunk], BOUNDS[st + 1][chunk + 1]
+        if whole:
+            if chunk == 0:
+                loads[st].wait()
+            wait_rows(st, hi + 1, True)
+        wait_rows(st, hi + 1, False)
+        if whole:
+            return conv(bufs[st], (wb1, wb2)[st], lo, hi, (0, 1, 2))
+        x = conv(bufs[st], (wb1, wb2)[st], lo, hi, (2 * core,))
+        return [v + acc[st, 16 * lo : 16 * hi, 128 * n : 128 * (n + 1)] for n, v in enumerate(x)]
+
+    def conv1(chunk, whole=False):
         lo, hi = CONV1[chunk], CONV1[chunk + 1]
-        wait_rows(0, hi + 1, True)
-        wait_rows(0, hi + 1, False)
-        x = conv(p1, wb1, lo, hi)
+        x = conv_far(0, chunk, whole)
         x = [v + off1[:, 128 * n : 128 * (n + 1)] for n, v in enumerate(x)]
         acts = pair_norm_silu(*x, gain2, inside_mask(lo, 16 * (hi - lo)))
         for n in range(3):
             p2[1, 16 * lo : 16 * hi, 128 * n : 128 * (n + 1)] = acts[n]
         send_rows(1, chunk)
 
-    def conv2(chunk):
-        if chunk == 0:
-            loads[1].wait()
+    def conv2(chunk, whole=False):
         lo, hi = CONV2[chunk], CONV2[chunk + 1]
-        wait_rows(1, hi + 1, True)
-        wait_rows(1, hi + 1, False)
-        x = conv(p2, wb2, lo, hi)
+        x = conv_far(1, chunk, whole)
         inside = inside_mask(lo, 16 * (hi - lo))
         for n in range(3):
             lanes = slice(128 * n, 128 * (n + 1))
             v = xin[16 * lo : 16 * hi, lanes].astype(F32) + (x[n] + off2[:, lanes])
-            p3[1, 16 * lo : 16 * hi, lanes] = jnp.where(inside, v, 0.0).astype(BF16)
+            p3[1, 16 * lo : 16 * hi, lanes] = inside(v).astype(BF16)
         send_rows(2, chunk)
 
     def upsample(chunk, half):
@@ -349,7 +366,13 @@
                     mixed[pl.ds(at + a, n, stride=2), :] = recvb[half, zz, f, first:last, :].astype(F32)
                 out_ref[f, 192 * zz + 2 * first : 192 * zz + 2 * last, :] = mixed[at : at + 2 * n, :].astype(BF16)
 
-    work = (act1, conv1, conv2, lambda c: upsample(c, 0), lambda c: upsample(c, 1), interleave)
+    work = (
+        act1,
+        lambda c: conv_near(0, c), conv1,
+        lambda c: conv_near(1, c), conv2,
+        lambda c: upsample(c, 0), lambda c: upsample(c, 1), interleave,
+        lambda c: conv1(c, True), lambda c: conv2(c, True),
+    )
     for stage_chunk in ORDER.split():
         work[int(stage_chunk[0])](int(stage_chunk[1]))
 
@@ -382,6 +405,7 @@
             weights, weights,
             pltpu.VMEM((2, 1280, 256), BF16),
             pltpu.VMEM((2, 1280, 256), BF16),
+            pltpu.VMEM((2, 16 * PAIRS, 384), F32),
             pltpu.VMEM((2, 16 * 96, 128), F32),
             pltpu.VMEM((2, 16, 96, 128), BF16),
             pltpu.VMEM((2, 4, 4, 96, 128), BF16),

time: 37.1 us -> 36.6 us (0.987)
  Pallas kernels: 36.1 us -> 35.6 us
    pallas_call x1, Pallas kernels: 36.1 us -> 35.6 us  [shards(): pl.pallas_call(kernel, out_shape=pltpu.VMEM((4, 768, 128), BF16), in_spec...]
where the time goes in v5:
time: 36.6 us; the launch traced here: 36.5 us
  Pallas kernels  35.6 us (97%)
  local copies, waits for them, and re-layouts  0.88 us (2%)
    pallas_call x1, Pallas kernels, shards(): pl.pallas_call(kernel, out_shape=pltpu.VMEM((4, 768, 128), BF16), in_spec...  35.6 us
    unnamed x1, local copies, waits for them, and re-layouts  0.88 us

profile of v5, /device:TPU:7, one launch (start us, length us, event | category | flops | bytes accessed | tf_op | source)
XLA Modules:
  0.0 36.5 jit_solution(5740083152089669433)
XLA Ops:
  0.0 35.6 %shard_map.91 = bf16[4,768,128]{2,1,0:T(8,128)(2,1)S(1)} custom-call(bf16[1536,128]{1,0:T(8,128)(2,1)} %bitcast.20, bf16[3,3,576,192]{3,2,1,0:T(8,128)(2,1)} %bitcast.18, bf16[3,3,576,192]{3,2,1,0:T(8,128)(2,1)} %bitcast.19, bf16[3,3,192,96]{3,2,1,0:T(8,128)(2,1)} %up_ref.1, f32[1,192]{1,0:T(1,128)} %bitcast.21, f32[1,192]{1,0:T(1,128)} %bitcast.22, ...), custom_call_target="tpu_custom_call" | custom-call | tf_op jit(solution)/shard_map/pallas_call | solution.py:396
  35.6 0.9 %copy.13 = bf16[4,2,49152]{2,1,0:T(2,128)(2,1)} copy(bf16[4,2,49152]{2,1,0:T(2,128)(2,1)S(1)} %bitcast.17) | data formatting | bytes 1572864

commit v6 on v5

--- a/solution.py
+++ b/solution.py
@@ -129,7 +129,7 @@
         return zz, local, remote
 
     for chunk in range(COUNTS[0]):
-        for ahead in (2, 1, 3, 0):
+        for ahead in (1, 3, 2, 0):
             for fits, lo, hi in windows(chunk):
                 zz, local, remote = reshard(chunk, ahead, lo, hi)
                 if ahead == 0:

time: 36.6 us -> 36.6 us (level)
  no operation moved by 1% of the time
where the time goes in v6:
time: 36.6 us; the launch traced here: 36.5 us
  Pallas kernels  35.6 us (97%)
  local copies, waits for them, and re-layouts  0.88 us (2%)
    pallas_call x1, Pallas kernels, shards(): pl.pallas_call(kernel, out_shape=pltpu.VMEM((4, 768, 128), BF16), in_spec...  35.6 us
    unnamed x1, local copies, waits for them, and re-layouts  0.88 us

profile of v6, /device:TPU:7, one launch (start us, length us, event | category | flops | bytes accessed | tf_op | source)
XLA Modules:
  0.0 36.5 jit_solution(4060807216053056796)
XLA Ops:
  0.0 35.6 %shard_map.91 = bf16[4,768,128]{2,1,0:T(8,128)(2,1)S(1)} custom-call(bf16[1536,128]{1,0:T(8,128)(2,1)} %bitcast.20, bf16[3,3,576,192]{3,2,1,0:T(8,128)(2,1)} %bitcast.18, bf16[3,3,576,192]{3,2,1,0:T(8,128)(2,1)} %bitcast.19, bf16[3,3,192,96]{3,2,1,0:T(8,128)(2,1)} %up_ref.1, f32[1,192]{1,0:T(1,128)} %bitcast.21, f32[1,192]{1,0:T(1,128)} %bitcast.22, ...), custom_call_target="tpu_custom_call" | custom-call | tf_op jit(solution)/shard_map/pallas_call | solution.py:396
  35.7 0.9 %copy.13 = bf16[4,2,49152]{2,1,0:T(2,128)(2,1)} copy(bf16[4,2,49152]{2,1,0:T(2,128)(2,1)S(1)} %bitcast.17) | data formatting | bytes 1572864
